TPU v7x, 256 devices: a whole 4x4x8 slice. The times are simulated.
256 devices in a mesh: slab: 64 (over z, x, core), blk: 4 (over y).
Axes of the slice: x: 4, y: 4, z: 8, core: 2. Of those that a mesh axis runs over, the one named last changes fastest.
Arguments:
- volume: bfloat16 [64, 12, 48, 2, 4096], P('slab', 'blk'), may hold values from -6 to 6
- tissue: int32 [64, 12], P('slab', 'blk'), may hold values from 0 to 1
- face_owner: int32 [2, 12, 2, 1], P(None, 'blk'), may hold values from 0 to 3; in each aligned block of 6 rows (0 to 5, 6 to 11, ..., all dimensions but the last counted through in order) at most 3 rows name the same one
- face_slot: int32 [2, 12, 2], P(None, 'blk'), may hold values from 0 to 2
- plane_weight: bfloat16 [48, 432], replicated, may hold values from -0.3125 to 0.3125
- depth_weight: bfloat16 [48, 144], replicated, may hold values from -0.5 to 0.5
- norm_gain: float32 [48], replicated, may hold values from 0.5 to 1.5
- norm_bias: float32 [48], replicated, may hold values from -3 to 3
Outputs:
- features_out: bfloat16 [64, 12, 48, 2, 4096], P('slab', 'blk')
Inputs may be any that keep to these rules, and one draw needn't show every extreme that they name: `face_owner`: among the (6) entries of one device for one orientation (its blocks, both sides), no device is named more than 3 times, and in every draw some device is named exactly 3 times.
All inputs are finite; a program needn't handle non-finite values.
Results may differ from a plain program's by a relative error of at most 0.005.
Values may be sent and summed in bfloat16 or wider, within the bound.
No kernel may reach another device: no remote copies, remote signals or barrier semaphores. Data moves between devices by JAX's collectives and lax.ppermute only.
A program may use at most 128 MiB of HBM per device.

v0:
```python
import functools
import jax
import jax.numpy as jnp
from jax import lax
from jax.sharding import PartitionSpec as P
import jax.experimental.pallas as pl
import jax.experimental.pallas.tpu as pltpu

LANES = 128
SLOTS = 3
BF = jnp.bfloat16
F32 = jnp.float32
VM = pl.BlockSpec(memory_space=pltpu.VMEM)
SM = pl.BlockSpec(memory_space=pltpu.SMEM)
HB = pl.BlockSpec(memory_space=pltpu.HBM)


def lane_ids(rows):
    return lax.broadcasted_iota(jnp.int32, (rows, LANES), 1)


def roll(x, k):
    return pltpu.roll(x, k % LANES, 1)


def params(mib):
    return pltpu.CompilerParams(vmem_limit_bytes=mib * 2**20)


def split_kernel(side_ref, me_ref, vol_ref, live_ref, near_ref, far_ref, strip_ref, kept_ref, live_s, sems, live_sem):
    c, n = near_ref.shape[1:]
    copies = [pltpu.make_async_copy(vol_ref.at[0, b], kept_ref.at[b], sems.at[b]) for b in range(SLOTS)]
    for copy in copies:
        copy.start()
    lives = pltpu.make_async_copy(live_ref, live_s, live_sem)
    lives.start()
    side = side_ref[0]
    i = lax.broadcasted_iota(jnp.int32, (2 * c, 2 * c), 0)
    j = lax.broadcasted_iota(jnp.int32, (2 * c, 2 * c), 1)
    order = jnp.where(j == jnp.where(i < c, 2 * i + 1 - side, 2 * (i - c) + side), 1.0, 0.0).astype(BF)
    lane = lane_ids(2 * c)
    lives.wait()
    for b in range(SLOTS):
        copies[b].wait()
        x = kept_ref[b].reshape(2 * c, n)
        d = jnp.dot(order, x, preferred_element_type=F32).astype(BF)
        near_ref[b] = d[:c]
        far_ref[b] = d[c:]
        live = jnp.where(live_s[0, b] > 0, 1.0, 0.0).astype(BF)
        rows = jnp.where(lane < 64, d[:, :LANES], d[:, n - LANES:])
        cols = jnp.zeros((2 * c, LANES), BF)
        for t in range(n // LANES):
            tile = d[:, t * LANES:(t + 1) * LANES]
            cols = jnp.where(lane % 64 == 2 * t, roll(tile, 2 * t - 63), cols)
            cols = jnp.where(lane % 64 == (2 * t + 63) % 64, roll(tile, 2 * t + 63), cols)
        rows = rows * live
        cols = cols * live
        for q in range(2):
            strip_ref[q, b, 0] = rows[q * c:(q + 1) * c]
            strip_ref[q, b, 1] = cols[q * c:(q + 1) * c]


def split(side, me, vol, tissue):
    _, s, c, z, n = vol.shape
    return pl.pallas_call(
        split_kernel, name="split",
        in_specs=[SM, SM, HB, HB], out_specs=[VM] * 4,
        out_shape=[jax.ShapeDtypeStruct((s, c, n), BF)] * 2
        + [jax.ShapeDtypeStruct((2, s, 2, c, LANES), BF),
           jax.ShapeDtypeStruct((s, c, z, n), BF)],
        scratch_shapes=[pltpu.SMEM((1, s), jnp.int32), pltpu.SemaphoreType.DMA((SLOTS,)), pltpu.SemaphoreType.DMA],
        compiler_params=params(24),
    )(side, me, pltpu.with_memory_space_constraint(vol, pltpu.HBM), pltpu.with_memory_space_constraint(tissue, pltpu.HBM))


def conv_layer(x_at, rows, cols, weight, stack, emit):
    c = rows.shape[0]
    tiles = stack.shape[1] // LANES - 1
    lane = lane_ids(c)
    first = lane % 64 == 0
    last = lane % 64 == 63
    low = lane < 64
    for t in range(tiles + 1):
        at = slice(t * LANES, (t + 1) * LANES)
        tile = x_at(t) if t < tiles else rows
        edge = roll(cols, -2 * t) if t < tiles else jnp.zeros((c, LANES), BF)
        stack[0:c, at] = jnp.where(first, edge, roll(tile, 1))
        stack[c:2 * c, at] = tile
        stack[2 * c:, at] = jnp.where(last, edge, roll(tile, -1))

    def mix(start, size):
        return jnp.dot(weight, stack[:, start:start + size], preferred_element_type=F32)

    outer = mix(tiles * LANES, LANES)
    above, end = outer[:c], outer[2 * c:]
    middle = turned = None
    for pair in range(tiles // 2):
        u = mix(pair * 2 * LANES, 2 * LANES)
        for h in range(2):
            part = u[:, h * LANES:(h + 1) * LANES]
            turn = roll(above + part[2 * c:], 64)
            t = 2 * pair + h
            if t:
                emit(t - 1, middle + jnp.where(low, turned, turn))
            above, middle, turned = part[:c], part[c:2 * c], turn
    turn = roll(above + end, 64)
    emit(tiles - 1, middle + jnp.where(low, turned, turn))


def tap_rows(weight):
    width = weight.shape[1] // 3
    return jnp.concatenate([weight[:, a * width:(a + 1) * width] for a in range(3)], axis=0)


def column(row):
    c = row.shape[1]
    i = lax.broadcasted_iota(jnp.int32, (c, c), 0)
    j = lax.broadcasted_iota(jnp.int32, (c, c), 1)
    return jnp.sum(jnp.where(i == j, jnp.broadcast_to(row, (c, c)), 0.0), axis=1, keepdims=True)


def own_kernel(me_ref, live_ref, owner_ref, slot_ref, weight_ref, gain_ref, bias_ref, near_ref, far_ref,
               own_ref, one_ref, two_ref, three_ref, near_act, far_act, note_ref, table, plane, stack):
    c, n = near_ref.shape[1:]
    lane = lane_ids(c)
    me = me_ref[0]
    for k, ref in enumerate((own_ref, one_ref, two_ref, three_ref)):
        table[k] = ref[...]
    weight = tap_rows(weight_ref[...])
    gain_col = column(gain_ref[...])
    bias_col = column(bias_ref[...])
    scale = 1.0 / (2 * n)
    note = jnp.zeros((c, LANES), F32)

    def pick(t, b, e):
        return lax.rem(me - owner_ref[t, e, 0, b] + 4, 4), slot_ref[t, e, b]

    for b in range(SLOTS):
        south, north, west, east = pick(0, b, 1), pick(0, b, 0), pick(1, b, 0), pick(1, b, 1)
        total = [jnp.zeros((c, LANES), F32)]
        for q, ref in enumerate((near_ref, far_ref)):
            rows = jnp.where(lane < 64, table[south[0], q, south[1], 0], table[north[0], q, north[1], 0])
            cols = jnp.where(lane % 2 == 0, table[west[0], q, west[1], 1], table[east[0], q, east[1], 1])
            if q == 1:
                note_ref[2 * b] = rows
                note_ref[2 * b + 1] = cols

            def emit(t, value, q=q):
                plane[q, :, t * LANES:(t + 1) * LANES] = value
                total[0] += value
            conv_layer(lambda t: ref[b, :, t * LANES:(t + 1) * LANES], rows, cols, weight, stack, emit)
        mean = jnp.sum(total[0], axis=1, keepdims=True) * scale
        mean_b = jnp.broadcast_to(mean, (c, LANES))
        square = jnp.zeros((c, LANES), F32)
        for q in range(2):
            for t in range(n // LANES):
                dev = plane[q, :, t * LANES:(t + 1) * LANES] - mean_b
                square += dev * dev
        var = jnp.sum(square, axis=1, keepdims=True) * scale
        live = jnp.where(live_ref[0, b] > 0, 1.0, 0.0)
        gain_b = jnp.broadcast_to(lax.rsqrt(var + 1e-05) * gain_col * live, (c, LANES))
        bias_b = jnp.broadcast_to(bias_col * live, (c, LANES))
        for q, out in enumerate((near_act, far_act)):
            for t in range(n // LANES):
                at = slice(t * LANES, (t + 1) * LANES)
                out[b, :, at] = jnp.maximum((plane[q, :, at] - mean_b) * gain_b + bias_b, 0.0).astype(BF)
        for k, value in enumerate((mean_b, gain_b, bias_b)):
            note = jnp.where(lane == 3 * b + k, value, note)
    for k in range(3):
        part = note.astype(BF)
        note_ref[2 * SLOTS + k] = part
        note = note - part.astype(F32)


def own_layers(me, live, owner, slot, weight, gain, bias, near, far, strips):
    s, c, n = near.shape
    return pl.pallas_call(
        own_kernel, name="own",
        in_specs=[SM] * 4 + [VM] * 9, out_specs=[VM] * 3,
        out_shape=[jax.ShapeDtypeStruct((s, c, n), BF)] * 2 + [jax.ShapeDtypeStruct((2 * s + 3, c, LANES), BF)],
        scratch_shapes=[pltpu.VMEM((4,) + strips[0].shape, BF), pltpu.VMEM((2, c, n), F32),
                        pltpu.VMEM((3 * c, n + LANES), BF)],
        compiler_params=params(16),
    )(me, live, owner, slot, weight, gain, bias, near, far, *strips)


def final_kernel(side_ref, live_ref, weight_ref, depth_ref, kept_ref, raw_ref, note_ref, near_in_ref, near_ref, far_ref,
                 out_ref, stack, taps, done, sems):
    c, n = near_ref.shape[1:]
    side = side_ref[0]
    weight = tap_rows(weight_ref[...])
    k = lax.broadcasted_iota(jnp.int32, (3 * c, 4 * c), 0)
    j = lax.broadcasted_iota(jnp.int32, (3 * c, 4 * c), 1)
    oi = lax.broadcasted_iota(jnp.int32, (2 * c, c), 0)
    oj = lax.broadcasted_iota(jnp.int32, (2 * c, c), 1)
    depth = jnp.zeros((2 * c, 4 * c), F32)
    for z in range(2):
        layer = k // c + z
        place = jnp.where(side > 0, layer, 3 - layer) * c + k % c
        spread = jnp.where(j == place, 1.0, 0.0).astype(BF)
        part = jnp.dot(depth_ref[...], spread, preferred_element_type=F32).astype(BF)
        pick = jnp.where(oi == 2 * oj + z, 1.0, 0.0).astype(BF)
        depth += jnp.dot(pick, part, preferred_element_type=F32)
    depth = depth.astype(BF)
    stats = note_ref[2 * SLOTS].astype(F32) + note_ref[2 * SLOTS + 1].astype(F32) + note_ref[2 * SLOTS + 2].astype(F32)
    wide = 512
    copies = []
    for b in range(SLOTS):
        mean, gain, bias = (jnp.broadcast_to(stats[:, 3 * b + i:3 * b + i + 1], (c, LANES)) for i in range(3))

        def emit(t, value):
            stack[3 * c:, t * LANES:(t + 1) * LANES] = jnp.maximum((value - mean) * gain + bias, 0.0).astype(BF)
        conv_layer(lambda t: raw_ref[b, :, t * LANES:(t + 1) * LANES], note_ref[2 * b], note_ref[2 * b + 1],
                   weight, taps, emit)
        stack[0:c] = near_in_ref[b]
        stack[c:2 * c] = near_ref[b]
        stack[2 * c:3 * c] = far_ref[b]
        live = jnp.where(live_ref[0, b] > 0, 1.0, 0.0)
        for w in range(n // wide):
            at = slice(w * wide, (w + 1) * wide)
            mixed = jnp.dot(depth, stack[:, at], preferred_element_type=F32)
            given = kept_ref[b, :, :, at].reshape(2 * c, wide).astype(F32)
            done[b, :, :, at] = ((given + mixed) * live).astype(BF).reshape(c, 2, wide)
        copies.append(pltpu.make_async_copy(done.at[b], out_ref.at[0, b], sems.at[b]))
        copies[-1].start()
    for copy in copies:
        copy.wait()


def final(side, live, weight, depth, kept, raw, note, near_in, near, far):
    s, c, z, n = kept.shape
    return pl.pallas_call(
        final_kernel, name="final",
        in_specs=[SM] * 2 + [VM] * 8, out_specs=HB,
        out_shape=jax.ShapeDtypeStruct((1, s, c, z, n), BF),
        scratch_shapes=[pltpu.VMEM((4 * c, n), BF), pltpu.VMEM((3 * c, n + LANES), BF), pltpu.VMEM((s, c, z, n), BF),
                        pltpu.SemaphoreType.DMA((SLOTS,))],
        compiler_params=params(16),
    )(side, live, weight, depth, kept, raw, note, near_in, near, far)


def swap(value, axis, first):
    count = lax.axis_size(axis)
    pairs = []
    for i in range(first, count - 1, 2):
        pairs += [(i, i + 1), (i + 1, i)]
    return lax.ppermute(value, axis, pairs)


def ring(value, axis, steps):
    count = lax.axis_size(axis)
    return lax.ppermute(value, axis, [(i, (i + steps) % count) for i in range(count)])


def body(volume, tissue, face_owner, face_slot, plane_weight, depth_weight, norm_gain, norm_bias):
    owner = jnp.transpose(face_owner, (0, 2, 3, 1))
    slot = jnp.transpose(face_slot, (0, 2, 1))
    gain = norm_gain.reshape(1, -1)
    bias = norm_bias.reshape(1, -1)
    me = lax.axis_index("blk").reshape(1)
    side = (lax.axis_index("slab") % 2).reshape(1)
    near, far, strips, kept = split(side, me, volume, tissue)
    raw = swap(far, "slab", 1)
    strips = [strips] + [ring(strips, "blk", k) for k in (1, 2, 3)]
    near_act, far_act, note = own_layers(me, tissue, owner, slot, plane_weight, gain, bias, near, far, strips)
    note_in = swap(note, "slab", 1)
    near_in = swap(near_act, "slab", 0)
    return final(side, tissue, plane_weight, depth_weight, kept, raw, note_in, near_in, near_act, far_act)


def solution(mesh):
    return jax.shard_map(
        body,
        mesh=mesh,
        in_specs=(
            P("slab", "blk", None, None, None),
            P("slab", "blk"),
            P(None, "blk", None, None),
            P(None, "blk", None),
            P(),
            P(),
            P(),
            P(),
        ),
        out_specs=P("slab", "blk", None, None, None),
        check_vma=False,
    )
```

profile of v0, /device:TPU:103, one launch (start us, length us, event | category | flops | bytes accessed | tf_op | source)
XLA Modules:
  0.0 40.1 jit_solution(14538443242892790299)
XLA Ops:
  0.0 0.0 copy-start
  0.0 0.0 copy-start.2
  0.0 0.0 copy-start.3
  0.0 0.0 copy-start.4
  0.0 0.0 copy-start.5
  0.0 0.0 copy-start.6
  0.0 3.3 %split.1 = (bf16[3,48,4096]{2,1,0:T(8,128)(2,1)S(1)}, bf16[3,48,4096]{2,1,0:T(8,128)(2,1)S(1)}, bf16[2,3,2,48,128]{4,3,2,1,0:T(8,128)(2,1)S(1)}, bf16[3,48,2,4096]{3,2,1,0:T(2,128)(2,1)S(1)}) custom-call(s32[1]{0:T(128)} %bitcast.side_ref, s32[1]{0:T(128)} %bitcast.1.me_ref, bf16[1,3,48,2,4096]{4,3,2,1,0:T(2,128)(2,1)} %vol_ref.1, s32[1,3]{1,0:T(1,128)} %live_ref.5), custom_call_target="tpu_custom_call" | custom-call | tf_op jit(solution)/shard_map/split/pallas_call | solution.py:65
  3.3 2.8 %collective-permute-start.3 = (bf16[2,3,2,48,128]{4,3,2,1,0:T(8,128)(2,1)S(1)}, bf16[2,3,2,48,128]{4,3,2,1,0:T(8,128)(2,1)S(1)}, u32[]{:S(2)}, u32[]{:S(2)}) collective-permute-start(bf16[2,3,2,48,128]{4,3,2,1,0:T(8,128)(2,1)S(1)} %get-tuple-element.15.own_ref), channel_id=1, source_target_pairs={{0,3},{1,0},{2,1},{3,2},{4,7},{5,4},{6,5},{7,6},{8,11},{9,8},{10,9... | collective-permute-start | bytes 442376 | tf_op jit(solution)/shard_map/ppermute | solution.py:252
  6.1 0.3 collective-permute-start.2
  6.5 0.7 %collective-permute-start.1 = (bf16[2,3,2,48,128]{4,3,2,1,0:T(8,128)(2,1)S(1)}, bf16[2,3,2,48,128]{4,3,2,1,0:T(8,128)(2,1)S(1)}, u32[]{:S(2)}, u32[]{:S(2)}) collective-permute-start(bf16[2,3,2,48,128]{4,3,2,1,0:T(8,128)(2,1)S(1)} %get-tuple-element.15.own_ref), channel_id=1, source_target_pairs={{0,1},{1,2},{2,3},{3,0},{4,5},{5,6},{6,7},{7,4},{8,9},{9,10},{10,1... | collective-permute-start | bytes 442376 | tf_op jit(solution)/shard_map/ppermute | solution.py:252
  7.2 6.1 %collective-permute-start = (bf16[3,48,4096]{2,1,0:T(8,128)(2,1)S(1)}, bf16[3,48,4096]{2,1,0:T(8,128)(2,1)S(1)}, u32[]{:S(2)}, u32[]{:S(2)}) collective-permute-start(bf16[3,48,4096]{2,1,0:T(8,128)(2,1)S(1)} %get-tuple-element.13.far_ref), channel_id=1, source_target_pairs={{4,8},{8,4},{12,16},{16,12},{20,24},{24,20},{28,32},{32,28},{36,40... | collective-permute-start | bytes 3538952 | tf_op jit(solution)/shard_map/ppermute | solution.py:247
  13.2 0.0 collective-permute-done.3.three_ref
  13.3 0.0 collective-permute-done.2.two_ref
  13.3 3.3 %collective-permute-done.1.one_ref = bf16[2,3,2,48,128]{4,3,2,1,0:T(8,128)(2,1)S(1)} collective-permute-done((bf16[2,3,2,48,128]{4,3,2,1,0:T(8,128)(2,1)S(1)}, bf16[2,3,2,48,128]{4,3,2,1,0:T(8,128)(2,1)S(1)}, u32[]{:S(2)}, u32[]{:S(2)}) %collective-permute-start.1) | collective-permute-done | bytes 147488 | tf_op jit(solution)/shard_map/ppermute | solution.py:252
  16.6 0.0 copy-done
  16.6 0.0 copy-done.2
  16.6 0.0 copy-done.3
  16.6 0.0 copy-done.4
  16.6 0.0 copy-done.5
  16.6 0.0 copy-done.6
  16.6 0.0 copy-start.1
  16.6 7.4 %own.1 = (bf16[3,48,4096]{2,1,0:T(8,128)(2,1)S(1)}, bf16[3,48,4096]{2,1,0:T(8,128)(2,1)S(1)}, bf16[9,48,128]{2,1,0:T(8,128)(2,1)S(1)}) custom-call(s32[1]{0:T(128)} %bitcast.1.me_ref, s32[1,3]{1,0:T(1,128)S(1)} %copy-done.2, s32[2,2,1,3]{3,2,1,0:T(1,128)S(1)} %bitcast.6, s32[2,2,3]{2,1,0:T(2,128)S(1)} %bitcast.7, bf16[48,432]{1,0:T(8,128)(2,1)S(1)} %copy-done, ...), custom_call_target="tpu_custom_call" | custom-call | tf_op jit(solution)/shard_map/own/pallas_call | solution.py:177
  24.1 0.6 %collective-permute-start.5 = (bf16[3,48,4096]{2,1,0:T(8,128)(2,1)S(1)}, bf16[3,48,4096]{2,1,0:T(8,128)(2,1)S(1)}, u32[]{:S(2)}, u32[]{:S(2)}) collective-permute-start(bf16[3,48,4096]{2,1,0:T(8,128)(2,1)S(1)} %get-tuple-element.17.near_ref), channel_id=1, source_target_pairs={{0,4},{4,0},{8,12},{12,8},{16,20},{20,16},{24,28},{28,24},{32,36},... | collective-permute-start | bytes 3538952 | tf_op jit(solution)/shard_map/ppermute | solution.py:247
  24.6 4.8 %collective-permute-start.4 = (bf16[9,48,128]{2,1,0:T(8,128)(2,1)S(1)}, bf16[9,48,128]{2,1,0:T(8,128)(2,1)S(1)}, u32[]{:S(2)}, u32[]{:S(2)}) collective-permute-start(bf16[9,48,128]{2,1,0:T(8,128)(2,1)S(1)} %get-tuple-element.16), channel_id=1, source_target_pairs={{4,8},{8,4},{12,16},{16,12},{20,24},{24,20},{28,32},{32,28},{36,40... | collective-permute-start | bytes 331784 | tf_op jit(solution)/shard_map/ppermute | solution.py:247
  29.4 4.6 %collective-permute-done.4.note_ref = bf16[9,48,128]{2,1,0:T(8,128)(2,1)S(1)} collective-permute-done((bf16[9,48,128]{2,1,0:T(8,128)(2,1)S(1)}, bf16[9,48,128]{2,1,0:T(8,128)(2,1)S(1)}, u32[]{:S(2)}, u32[]{:S(2)}) %collective-permute-start.4) | collective-permute-done | bytes 110624 | tf_op jit(solution)/shard_map/ppermute | solution.py:247
  34.0 0.0 collective-permute-done.raw_ref
  34.0 0.0 collective-permute-done.5.near_in_ref
  34.0 0.0 copy-done.1
  34.0 5.9 %final.1 = bf16[1,3,48,2,4096]{4,3,2,1,0:T(2,128)(2,1)} custom-call(s32[1]{0:T(128)} %bitcast.side_ref, s32[1,3]{1,0:T(1,128)S(1)} %copy-done.2, bf16[48,432]{1,0:T(8,128)(2,1)S(1)} %copy-done, bf16[48,144]{1,0:T(8,128)(2,1)S(1)} %copy-done.1, bf16[3,48,2,4096]{3,2,1,0:T(2,128)(2,1)S(1)} %get-tuple-element.12.kept_ref, ...), custom_call_target="tpu_custom_call" | custom-call | tf_op jit(solution)/shard_map/final/pallas_call | solution.py:232
Async XLA Ops:
  0.0 16.6 %copy-start = (bf16[48,432]{1,0:T(8,128)(2,1)S(1)}, bf16[48,432]{1,0:T(8,128)(2,1)}, u32[]{:S(2)}) copy-start(bf16[48,432]{1,0:T(8,128)(2,1)} %weight_ref.3) | copy-start | bytes 124420
  0.0 16.6 %copy-start.2 = (s32[1,3]{1,0:T(1,128)S(1)}, s32[1,3]{1,0:T(1,128)}, u32[]{:S(2)}) copy-start(s32[1,3]{1,0:T(1,128)} %live_ref.5) | copy-start | bytes 40
  0.0 16.6 %copy-start.3 = (s32[2,3,2,1]{1,3,2,0:T(1,128)S(1)}, s32[2,3,2,1]{1,3,2,0:T(1,128)}, u32[]{:S(2)}) copy-start(s32[2,3,2,1]{1,3,2,0:T(1,128)} %param.10) | copy-start | bytes 148
  0.0 16.6 %copy-start.4 = (s32[2,3,2]{1,2,0:T(2,128)S(1)}, s32[2,3,2]{1,2,0:T(2,128)}, u32[]{:S(2)}) copy-start(s32[2,3,2]{1,2,0:T(2,128)} %param.11) | copy-start | bytes 148
  0.0 16.6 %copy-start.5 = (f32[48]{0:T(128)S(1)}, f32[48]{0:T(128)}, u32[]{:S(2)}) copy-start(f32[48]{0:T(128)} %param.14) | copy-start | bytes 580
  0.0 16.6 %copy-start.6 = (f32[48]{0:T(128)S(1)}, f32[48]{0:T(128)}, u32[]{:S(2)}) copy-start(f32[48]{0:T(128)} %param.15) | copy-start | bytes 580
  3.3 9.9 %collective-permute-start.3 = (bf16[2,3,2,48,128]{4,3,2,1,0:T(8,128)(2,1)S(1)}, bf16[2,3,2,48,128]{4,3,2,1,0:T(8,128)(2,1)S(1)}, u32[]{:S(2)}, u32[]{:S(2)}) collective-permute-start(bf16[2,3,2,48,128]{4,3,2,1,0:T(8,128)(2,1)S(1)} %get-tuple-element.15.own_ref), channel_id=1, source_target_pairs={{0,3},{1,0},{2,1},{3,2},{4,7},{5,4},{6,5},{7,6},{8,11},{9,8},{10,9... | collective-permute-start | bytes 442376 | tf_op jit(solution)/shard_map/ppermute | solution.py:252
  6.1 7.1 %collective-permute-start.2 = (bf16[2,3,2,48,128]{4,3,2,1,0:T(8,128)(2,1)S(1)}, bf16[2,3,2,48,128]{4,3,2,1,0:T(8,128)(2,1)S(1)}, u32[]{:S(2)}, u32[]{:S(2)}) collective-permute-start(bf16[2,3,2,48,128]{4,3,2,1,0:T(8,128)(2,1)S(1)} %get-tuple-element.15.own_ref), channel_id=1, source_target_pairs={{0,2},{1,3},{2,0},{3,1},{4,6},{5,7},{6,4},{7,5},{8,10},{9,11},{10,... | collective-permute-start | bytes 442376 | tf_op jit(solution)/shard_map/ppermute | solution.py:252
  6.5 10.1 %collective-permute-start.1 = (bf16[2,3,2,48,128]{4,3,2,1,0:T(8,128)(2,1)S(1)}, bf16[2,3,2,48,128]{4,3,2,1,0:T(8,128)(2,1)S(1)}, u32[]{:S(2)}, u32[]{:S(2)}) collective-permute-start(bf16[2,3,2,48,128]{4,3,2,1,0:T(8,128)(2,1)S(1)} %get-tuple-element.15.own_ref), channel_id=1, source_target_pairs={{0,1},{1,2},{2,3},{3,0},{4,5},{5,6},{6,7},{7,4},{8,9},{9,10},{10,1... | collective-permute-start | bytes 442376 | tf_op jit(solution)/shard_map/ppermute | solution.py:252
  7.2 26.8 %collective-permute-start = (bf16[3,48,4096]{2,1,0:T(8,128)(2,1)S(1)}, bf16[3,48,4096]{2,1,0:T(8,128)(2,1)S(1)}, u32[]{:S(2)}, u32[]{:S(2)}) collective-permute-start(bf16[3,48,4096]{2,1,0:T(8,128)(2,1)S(1)} %get-tuple-element.13.far_ref), channel_id=1, source_target_pairs={{4,8},{8,4},{12,16},{16,12},{20,24},{24,20},{28,32},{32,28},{36,40... | collective-permute-start | bytes 3538952 | tf_op jit(solution)/shard_map/ppermute | solution.py:247
  16.6 17.4 %copy-start.1 = (bf16[48,144]{1,0:T(8,128)(2,1)S(1)}, bf16[48,144]{1,0:T(8,128)(2,1)}, u32[]{:S(2)}) copy-start(bf16[48,144]{1,0:T(8,128)(2,1)} %depth_ref.1) | copy-start | bytes 41476
  24.1 10.0 %collective-permute-start.5 = (bf16[3,48,4096]{2,1,0:T(8,128)(2,1)S(1)}, bf16[3,48,4096]{2,1,0:T(8,128)(2,1)S(1)}, u32[]{:S(2)}, u32[]{:S(2)}) collective-permute-start(bf16[3,48,4096]{2,1,0:T(8,128)(2,1)S(1)} %get-tuple-element.17.near_ref), channel_id=1, source_target_pairs={{0,4},{4,0},{8,12},{12,8},{16,20},{20,16},{24,28},{28,24},{32,36},... | collective-permute-start | bytes 3538952 | tf_op jit(solution)/shard_map/ppermute | solution.py:247
  24.6 9.4 %collective-permute-start.4 = (bf16[9,48,128]{2,1,0:T(8,128)(2,1)S(1)}, bf16[9,48,128]{2,1,0:T(8,128)(2,1)S(1)}, u32[]{:S(2)}, u32[]{:S(2)}) collective-permute-start(bf16[9,48,128]{2,1,0:T(8,128)(2,1)S(1)} %get-tuple-element.16), channel_id=1, source_target_pairs={{4,8},{8,4},{12,16},{16,12},{20,24},{24,20},{28,32},{32,28},{36,40... | collective-permute-start | bytes 331784 | tf_op jit(solution)/shard_map/ppermute | solution.py:247
where the time goes:
time: 40.2 us; the launch traced here: 40.1 us
  Pallas kernels  16.6 us (41%)
  starting transfers between devices  15.2 us (38%)
  waiting for transfers between devices  7.93 us (20%)
    ppermute x3, starting transfers between devices, swap(): return lax.ppermute(value, axis, pairs)  11.4 us
    pallas_call x1, Pallas kernels, own_layers(): pl.pallas_call(own_kernel, name='own', in_specs=[SM] * 4 + [VM] * 9, out_...  7.45 us
    pallas_call x1, Pallas kernels, final(): pl.pallas_call(final_kernel, name='final', in_specs=[SM] * 2 + [VM] * 8,...  5.87 us
    ppermute x3, waiting for transfers between devices, swap(): return lax.ppermute(value, axis, pairs)  4.62 us
    ppermute x3, starting transfers between devices, ring(): lax.ppermute(value, axis, [(i, (i + steps) % count) for i in range(count)])  3.85 us
    ppermute x3, waiting for transfers between devices, ring(): lax.ppermute(value, axis, [(i, (i + steps) % count) for i in range(count)])  3.31 us
    pallas_call x1, Pallas kernels, split(): pl.pallas_call(split_kernel, name='split', in_specs=[SM, SM, HB, HB], out...  3.27 us
  transfers between devices with their start and end apart: 6, of which 2 were waited for; matrix products, arithmetic and copies ran while one was open for 0% of the time, Pallas kernels for 19%

commit v1 on v0

v1 whole, which is shorter than its diff:
```python
import functools
import jax
import jax.numpy as jnp
from jax import lax
from jax.sharding import PartitionSpec as P
import jax.experimental.pallas as pl
import jax.experimental.pallas.tpu as pltpu

LANES = 128
SLOTS = 3
BF = jnp.bfloat16
F32 = jnp.float32
VM = pl.BlockSpec(memory_space=pltpu.VMEM)
SM = pl.BlockSpec(memory_space=pltpu.SMEM)
HB = pl.BlockSpec(memory_space=pltpu.HBM)


def lane_ids(rows):
    return lax.broadcasted_iota(jnp.int32, (rows, LANES), 1)


def roll(x, k):
    return pltpu.roll(x, k % LANES, 1)


def params(mib):
    return pltpu.CompilerParams(vmem_limit_bytes=mib * 2**20)


def cost(us):
    return pl.CostEstimate(flops=us * 1_000_000_000, bytes_accessed=us * 1_000_000, transcendentals=0)


def split_kernel(side_ref, me_ref, vol_ref, live_ref, near_ref, far_ref, strip_ref, kept_ref, live_s, sems, live_sem):
    c, n = near_ref.shape[1:]
    copies = [pltpu.make_async_copy(vol_ref.at[0, b], kept_ref.at[b], sems.at[b]) for b in range(SLOTS)]
    for copy in copies:
        copy.start()
    lives = pltpu.make_async_copy(live_ref, live_s, live_sem)
    lives.start()
    side = side_ref[0]
    i = lax.broadcasted_iota(jnp.int32, (2 * c, 2 * c), 0)
    j = lax.broadcasted_iota(jnp.int32, (2 * c, 2 * c), 1)
    order = jnp.where(j == jnp.where(i < c, 2 * i + 1 - side, 2 * (i - c) + side), 1.0, 0.0).astype(BF)
    lane = lane_ids(2 * c)
    lives.wait()
    for b in range(SLOTS):
        copies[b].wait()
        x = kept_ref[b].reshape(2 * c, n)
        d = jnp.dot(order, x, preferred_element_type=F32).astype(BF)
        near_ref[b] = d[:c]
        far_ref[b] = d[c:]
        live = jnp.where(live_s[0, b] > 0, 1.0, 0.0).astype(BF)
        rows = jnp.where(lane < 64, d[:, :LANES], d[:, n - LANES:])
        cols = jnp.zeros((2 * c, LANES), BF)
        for t in range(n // LANES):
            tile = d[:, t * LANES:(t + 1) * LANES]
            cols = jnp.where(lane % 64 // 2 == t, roll(tile, 2 * t + 65), cols)
        rows = rows * live
        cols = cols * live
        for q in range(2):
            strip_ref[q, b, 0] = rows[q * c:(q + 1) * c]
            strip_ref[q, b, 1] = cols[q * c:(q + 1) * c]


def split(side, me, vol, tissue):
    _, s, c, z, n = vol.shape
    return pl.pallas_call(
        split_kernel, name="split",
        in_specs=[SM, SM, HB, HB], out_specs=[VM] * 4,
        out_shape=[jax.ShapeDtypeStruct((s, c, n), BF)] * 2
        + [jax.ShapeDtypeStruct((2, s, 2, c, LANES), BF),
           jax.ShapeDtypeStruct((s, c, z, n), BF)],
        scratch_shapes=[pltpu.SMEM((1, s), jnp.int32), pltpu.SemaphoreType.DMA((SLOTS,)), pltpu.SemaphoreType.DMA],
        compiler_params=params(24),
    )(side, me, pltpu.with_memory_space_constraint(vol, pltpu.HBM), pltpu.with_memory_space_constraint(tissue, pltpu.HBM))


def conv_layer(x_at, weight, stack, emit):
    c, n = weight.shape[0] // 3, stack.shape[1]
    tiles = n // LANES
    lane = lane_ids(c)
    zero = jnp.zeros((c, LANES), BF)
    low = lane < 64
    for t in range(tiles):
        at = slice(t * LANES, (t + 1) * LANES)
        tile = x_at(t)
        stack[0:c, at] = jnp.where(lane % 64 == 0, zero, roll(tile, 1))
        stack[c:2 * c, at] = tile
        stack[2 * c:, at] = jnp.where(lane % 64 == 63, zero, roll(tile, -1))
    above = jnp.zeros((c, LANES), F32)
    middle = turned = None
    for pair in range(tiles // 2):
        u = jnp.dot(weight, stack[:, pair * 2 * LANES:(pair + 1) * 2 * LANES], preferred_element_type=F32)
        for h in range(2):
            part = u[:, h * LANES:(h + 1) * LANES]
            turn = roll(above + part[2 * c:], 64)
            t = 2 * pair + h
            if t:
                emit(t - 1, middle + jnp.where(low, turned, turn))
            above, middle, turned = part[:c], part[c:2 * c], turn
    emit(tiles - 1, middle + jnp.where(low, turned, roll(above, 64)))


def edge_terms(rows, cols, weight):
    c = rows.shape[0]
    lane = lane_ids(c)
    zero = jnp.zeros((c, LANES), BF)
    low = lane < 64
    even = lane % 2 == 0
    row_taps = jnp.concatenate([jnp.where(lane % 64 == 0, zero, roll(rows, 1)), rows,
                                jnp.where(lane % 64 == 63, zero, roll(rows, -1))], axis=0)
    col_taps = jnp.concatenate([jnp.where(even, cols, zero), zero, jnp.where(even, zero, cols)], axis=0)
    u = jnp.dot(weight, jnp.concatenate([row_taps, col_taps], axis=1), preferred_element_type=F32)
    top = jnp.where(low, roll(u[:c, :LANES], 64), 0.0)
    bottom = jnp.where(low, 0.0, roll(u[2 * c:, :LANES], 64))
    v = u[:, LANES:]
    place = jnp.where(even, lane, (lane + 65) % LANES)
    upper = jnp.where(place < 64, jnp.where(place == 0, 0.0, roll(v[:c], 66)), roll(v[:c], 64))
    lower = jnp.where(place < 64, roll(v[2 * c:], 64), jnp.where(place == 126, 0.0, roll(v[2 * c:], 62)))
    return top, bottom, v[c:2 * c] + upper + lower


def with_edges(value, t, tiles, terms):
    top, bottom, strip = terms
    lane = lane_ids(value.shape[0])
    value = value + jnp.where((lane + 1) % 64 < 2, roll(strip, -2 * t), 0.0)
    if t == 0:
        value = value + top
    if t == tiles - 1:
        value = value + bottom
    return value


def tap_rows(weight):
    width = weight.shape[1] // 3
    return jnp.concatenate([weight[:, a * width:(a + 1) * width] for a in range(3)], axis=0)


def column(row):
    c = row.shape[1]
    i = lax.broadcasted_iota(jnp.int32, (c, c), 0)
    j = lax.broadcasted_iota(jnp.int32, (c, c), 1)
    return jnp.sum(jnp.where(i == j, jnp.broadcast_to(row, (c, c)), 0.0), axis=1, keepdims=True)


def bulk_kernel(weight_ref, near_ref, far_ref, plane_ref, sum_ref, stack):
    c, n = near_ref.shape[1:]
    weight = tap_rows(weight_ref[...])
    for b in range(SLOTS):
        total = [jnp.zeros((c, LANES), F32)]
        for q, ref in enumerate((near_ref, far_ref)):
            def emit(t, value):
                plane_ref[q, b, :, t * LANES:(t + 1) * LANES] = value
                total[0] += value
            conv_layer(lambda t: ref[b, :, t * LANES:(t + 1) * LANES], weight, stack, emit)
        sum_ref[b] = total[0]


def bulk(weight, near, far):
    s, c, n = near.shape
    return pl.pallas_call(
        bulk_kernel, name="bulk",
        in_specs=[VM] * 3, out_specs=[VM] * 2,
        out_shape=[jax.ShapeDtypeStruct((2, s, c, n), F32), jax.ShapeDtypeStruct((s, c, LANES), F32)],
        scratch_shapes=[pltpu.VMEM((3 * c, n), BF)],
        compiler_params=params(8), cost_estimate=cost(5),
    )(weight, near, far)


def own_kernel(me_ref, live_ref, owner_ref, slot_ref, weight_ref, gain_ref, bias_ref, plane_ref, sum_ref,
               own_ref, one_ref, two_ref, three_ref, near_act, far_act, note_ref, table, off, edge):
    c, n = near_act.shape[1:]
    tiles = n // LANES
    lane = lane_ids(c)
    me = me_ref[0]
    for k, ref in enumerate((own_ref, one_ref, two_ref, three_ref)):
        table[k] = ref[...]
    weight = tap_rows(weight_ref[...])
    gain_col = column(gain_ref[...])
    bias_col = column(bias_ref[...])
    scale = 1.0 / (2 * n)
    note = jnp.zeros((c, LANES), F32)

    def pick(t, b, e):
        return lax.rem(me - owner_ref[t, e, 0, b] + 4, 4), slot_ref[t, e, b]

    means, squares = [], []
    for b in range(SLOTS):
        south, north, west, east = pick(0, b, 1), pick(0, b, 0), pick(1, b, 0), pick(1, b, 1)
        total = sum_ref[b]
        terms = []
        for q in range(2):
            rows = jnp.where(lane < 64, table[south[0], q, south[1], 0], table[north[0], q, north[1], 0])
            cols = jnp.where(lane % 2 == 0, table[west[0], q, west[1], 1],
                             roll(table[east[0], q, east[1], 1], -2))
            if q == 1:
                note_ref[2 * b] = rows
                note_ref[2 * b + 1] = cols
            for k, term in enumerate(edge_terms(rows, cols, weight)):
                edge[b, q, k] = term
                total += term
        means.append(jnp.broadcast_to(jnp.sum(total, axis=1, keepdims=True) * scale, (c, LANES)))
    for b in range(SLOTS):
        square = jnp.zeros((c, LANES), F32)
        for q in range(2):
            terms = [edge[b, q, k] for k in range(3)]
            for t in range(tiles):
                at = slice(t * LANES, (t + 1) * LANES)
                value = with_edges(plane_ref[q, b, :, at], t, tiles, terms) - means[b]
                off[b, q, :, at] = value
                square += value * value
        squares.append(square)
    for b in range(SLOTS):
        var = jnp.sum(squares[b], axis=1, keepdims=True) * scale
        live = jnp.where(live_ref[0, b] > 0, 1.0, 0.0)
        gain_b = jnp.broadcast_to(lax.rsqrt(var + 1e-05) * gain_col * live, (c, LANES))
        bias_b = jnp.broadcast_to(bias_col * live, (c, LANES))
        for q, out in enumerate((near_act, far_act)):
            for t in range(tiles):
                at = slice(t * LANES, (t + 1) * LANES)
                out[b, :, at] = jnp.maximum(off[b, q, :, at] * gain_b + bias_b, 0.0).astype(BF)
        for k, value in enumerate((means[b], gain_b, bias_b)):
            note = jnp.where(lane == 3 * b + k, value, note)
    for k in range(3):
        part = note.astype(BF)
        note_ref[2 * SLOTS + k] = part
        note = note - part.astype(F32)


def own_layers(me, live, owner, slot, weight, gain, bias, plane, sums, strips):
    _, s, c, n = plane.shape
    return pl.pallas_call(
        own_kernel, name="own",
        in_specs=[SM] * 4 + [VM] * 9, out_specs=[VM] * 3,
        out_shape=[jax.ShapeDtypeStruct((s, c, n), BF)] * 2 + [jax.ShapeDtypeStruct((2 * s + 3, c, LANES), BF)],
        scratch_shapes=[pltpu.VMEM((4,) + strips[0].shape, BF), pltpu.VMEM((s, 2, c, n), F32),
                        pltpu.VMEM((s, 2, 3, c, LANES), F32)],
        compiler_params=params(12), cost_estimate=cost(0),
    )(me, live, owner, slot, weight, gain, bias, plane, sums, *strips)


def depth_matrix(side, depth):
    c = depth.shape[0]
    k = lax.broadcasted_iota(jnp.int32, (3 * c, 4 * c), 0)
    j = lax.broadcasted_iota(jnp.int32, (3 * c, 4 * c), 1)
    oi = lax.broadcasted_iota(jnp.int32, (2 * c, c), 0)
    oj = lax.broadcasted_iota(jnp.int32, (2 * c, c), 1)
    total = jnp.zeros((2 * c, 4 * c), F32)
    for z in range(2):
        layer = k // c + z
        place = jnp.where(side > 0, layer, 3 - layer) * c + k % c
        spread = jnp.where(j == place, 1.0, 0.0).astype(BF)
        part = jnp.dot(depth, spread, preferred_element_type=F32).astype(BF)
        pick = jnp.where(oi == 2 * oj + z, 1.0, 0.0).astype(BF)
        total += jnp.dot(pick, part, preferred_element_type=F32)
    return total.astype(BF)


def inner_kernel(side_ref, weight_ref, depth_ref, kept_ref, raw_ref, near_ref, far_ref, plane_ref, part_ref, matrix_ref,
                 stack, taps):
    c, n = near_ref.shape[1:]
    weight = tap_rows(weight_ref[...])
    depth = depth_matrix(side_ref[0], depth_ref[...])
    matrix_ref[...] = jnp.concatenate([depth[:, :c], depth[:, 3 * c:]], axis=1)
    mine = depth[:, c:3 * c]
    wide = 512
    for b in range(SLOTS):
        stack[0:c] = near_ref[b]
        stack[c:] = far_ref[b]
        for w in range(n // wide):
            at = slice(w * wide, (w + 1) * wide)
            part_ref[b, :, at] = (jnp.dot(mine, stack[:, at], preferred_element_type=F32)
                                  + kept_ref[b, :, :, at].reshape(2 * c, wide).astype(F32))

        def emit(t, value):
            plane_ref[b, :, t * LANES:(t + 1) * LANES] = value
        conv_layer(lambda t: raw_ref[b, :, t * LANES:(t + 1) * LANES], weight, taps, emit)


def inner(side, weight, depth, kept, raw, near, far):
    s, c, n = near.shape
    return pl.pallas_call(
        inner_kernel, name="inner",
        in_specs=[SM] + [VM] * 6, out_specs=[VM] * 3,
        out_shape=[jax.ShapeDtypeStruct((s, c, n), F32), jax.ShapeDtypeStruct((s, 2 * c, n), F32),
                   jax.ShapeDtypeStruct((2 * c, 2 * c), BF)],
        scratch_shapes=[pltpu.VMEM((2 * c, n), BF), pltpu.VMEM((3 * c, n), BF)],
        compiler_params=params(8), cost_estimate=cost(100),
    )(side, weight, depth, kept, raw, near, far)


def final_kernel(live_ref, weight_ref, matrix_ref, plane_ref, part_ref, note_ref, near_in_ref, out_ref, stack, done, edge, norm, sems):
    c, n = near_in_ref.shape[1:]
    tiles = n // LANES
    weight = tap_rows(weight_ref[...])
    matrix = matrix_ref[...]
    stats = note_ref[2 * SLOTS].astype(F32) + note_ref[2 * SLOTS + 1].astype(F32) + note_ref[2 * SLOTS + 2].astype(F32)
    wide = 512
    copies = []
    for b in range(SLOTS):
        for k, term in enumerate(edge_terms(note_ref[2 * b], note_ref[2 * b + 1], weight)):
            edge[b, k] = term
        for k in range(3):
            norm[b, k] = jnp.broadcast_to(stats[:, 3 * b + k:3 * b + k + 1], (c, LANES))
    for b in range(SLOTS):
        mean, gain, bias = (norm[b, k] for k in range(3))
        terms = [edge[b, k] for k in range(3)]
        stack[0:c] = near_in_ref[b]
        for t in range(tiles):
            at = slice(t * LANES, (t + 1) * LANES)
            value = with_edges(plane_ref[b, :, at], t, tiles, terms) - mean
            stack[c:, at] = jnp.maximum(value * gain + bias, 0.0).astype(BF)
        live = jnp.where(live_ref[0, b] > 0, 1.0, 0.0)
        for w in range(n // wide):
            at = slice(w * wide, (w + 1) * wide)
            mixed = jnp.dot(matrix, stack[:, at], preferred_element_type=F32)
            done[b, :, :, at] = ((part_ref[b, :, at] + mixed) * live).astype(BF).reshape(c, 2, wide)
        copies.append(pltpu.make_async_copy(done.at[b], out_ref.at[0, b], sems.at[b]))
        copies[-1].start()
    for copy in copies:
        copy.wait()


def final(live, weight, matrix, plane, part, note, near_in):
    s, c, n = near_in.shape
    return pl.pallas_call(
        final_kernel, name="final",
        in_specs=[SM] + [VM] * 6, out_specs=HB,
        out_shape=jax.ShapeDtypeStruct((1, s, c, 2, n), BF),
        scratch_shapes=[pltpu.VMEM((2 * c, n), BF), pltpu.VMEM((s, c, 2, n), BF),
                        pltpu.VMEM((s, 3, c, LANES), F32), pltpu.VMEM((s, 3, c, LANES), F32), pltpu.SemaphoreType.DMA((SLOTS,))],
        compiler_params=params(12), cost_estimate=cost(2),
    )(live, weight, matrix, plane, part, note, near_in)


def swap(value, axis, first):
    count = lax.axis_size(axis)
    pairs = []
    for i in range(first, count - 1, 2):
        pairs += [(i, i + 1), (i + 1, i)]
    return lax.ppermute(value, axis, pairs)


def ring(value, axis, steps):
    count = lax.axis_size(axis)
    return lax.ppermute(value, axis, [(i, (i + steps) % count) for i in range(count)])


def body(volume, tissue, face_owner, face_slot, plane_weight, depth_weight, norm_gain, norm_bias):
    owner = jnp.transpose(face_owner, (0, 2, 3, 1))
    slot = jnp.transpose(face_slot, (0, 2, 1))
    gain = norm_gain.reshape(1, -1)
    bias = norm_bias.reshape(1, -1)
    me = lax.axis_index("blk").reshape(1)
    side = (lax.axis_index("slab") % 2).reshape(1)
    near, far, strips, kept = split(side, me, volume, tissue)
    raw = swap(far, "slab", 1)
    strips = [strips] + [ring(strips, "blk", k) for k in (1, 2, 3)]
    plane, sums = bulk(plane_weight, near, far)
    near_act, far_act, note = own_layers(me, tissue, owner, slot, plane_weight, gain, bias, plane, sums, strips)
    note_in = swap(note, "slab", 1)
    near_in = swap(near_act, "slab", 0)
    far_plane, part, matrix = inner(side, plane_weight, depth_weight, kept, raw, near_act, far_act)
    return final(tissue, plane_weight, matrix, far_plane, part, note_in, near_in)


def solution(mesh):
    return jax.shard_map(
        body,
        mesh=mesh,
        in_specs=(
            P("slab", "blk", None, None, None),
            P("slab", "blk"),
            P(None, "blk", None, None),
            P(None, "blk", None),
            P(),
            P(),
            P(),
            P(),
        ),
        out_specs=P("slab", "blk", None, None, None),
        check_vma=False,
    )
```

time: 40.2 us -> 34.7 us (0.86)
  waiting for transfers between devices: 7.93 us -> 1.02 us
  starting transfers between devices: 15.2 us -> 16.1 us
    pallas_call x1 -> x3, Pallas kernels: 5.87 us -> 10.6 us  [the longest x1 3.56 us: final(): pl.pallas_call(final_kernel, name='final', in_specs=[SM] + [VM] * 6, out_...]
    ppermute x3, waiting for transfers between devices: 4.62 us -> 0.16 us  [swap(): return lax.ppermute(value, axis, pairs)]
    pallas_call x1, Pallas kernels: 7.45 us -> 3.79 us  [own_layers(): pl.pallas_call(own_kernel, name='own', in_specs=[SM] * 4 + [VM] * 9, out_...]
    ppermute x3, waiting for transfers between devices: 3.31 us -> 0.86 us  [ring(): lax.ppermute(value, axis, [(i, (i + steps) % count) for i in range(count)])]
    ppermute x3, starting transfers between devices: 3.85 us -> 5.06 us  [ring(): lax.ppermute(value, axis, [(i, (i + steps) % count) for i in range(count)])]
    pallas_call x1, Pallas kernels: 3.27 us -> 2.58 us  [split(): pl.pallas_call(split_kernel, name='split', in_specs=[SM, SM, HB, HB], out...]
  transfers between devices with their start and end apart: 6 -> 6, of which waited for: 2 -> 3; matrix products, arithmetic and copies ran while one was open for 0% -> 0% of each run, Pallas kernels for 19% -> 31%
where the time goes in v1:
time: 34.7 us; the launch traced here: 34.3 us
  Pallas kernels  16.9 us (49%)
  starting transfers between devices  16.1 us (46%)
  waiting for transfers between devices  1.02 us (3%)
    ppermute x3, starting transfers between devices, swap(): return lax.ppermute(value, axis, pairs)  11 us
    ppermute x3, starting transfers between devices, ring(): lax.ppermute(value, axis, [(i, (i + steps) % count) for i in range(count)])  5.06 us
    pallas_call x1, Pallas kernels, own_layers(): pl.pallas_call(own_kernel, name='own', in_specs=[SM] * 4 + [VM] * 9, out_...  3.79 us
    pallas_call x1, Pallas kernels, final(): pl.pallas_call(final_kernel, name='final', in_specs=[SM] + [VM] * 6, out_...  3.56 us
    pallas_call x1, Pallas kernels, inner(): pl.pallas_call(inner_kernel, name='inner', in_specs=[SM] + [VM] * 6, out_...  3.52 us
    pallas_call x1, Pallas kernels, bulk(): pl.pallas_call(bulk_kernel, name='bulk', in_specs=[VM] * 3, out_specs=[VM...  3.5 us
    pallas_call x1, Pallas kernels, split(): pl.pallas_call(split_kernel, name='split', in_specs=[SM, SM, HB, HB], out...  2.58 us
    ppermute x3, waiting for transfers between devices, ring(): lax.ppermute(value, axis, [(i, (i + steps) % count) for i in range(count)])  0.86 us
  transfers between devices with their start and end apart: 6, of which 3 were waited for; matrix products, arithmetic and copies ran while one was open for 0% of the time, Pallas kernels for 31%

profile of v1, /device:TPU:103, one launch (start us, length us, event | category | flops | bytes accessed | tf_op | source)
XLA Modules:
  0.0 34.3 jit_solution(11933914934890776243)
XLA Ops:
  0.0 0.0 copy-start
  0.0 2.6 %split.1 = (bf16[3,48,4096]{2,1,0:T(8,128)(2,1)S(1)}, bf16[3,48,4096]{2,1,0:T(8,128)(2,1)S(1)}, bf16[2,3,2,48,128]{4,3,2,1,0:T(8,128)(2,1)S(1)}, bf16[3,48,2,4096]{3,2,1,0:T(2,128)(2,1)S(1)}) custom-call(s32[1]{0:T(128)} %bitcast.side_ref, s32[1]{0:T(128)} %bitcast.1.me_ref, bf16[1,3,48,2,4096]{4,3,2,1,0:T(2,128)(2,1)} %vol_ref.1, s32[1,3]{1,0:T(1,128)} %live_ref.5), custom_call_target="tpu_custom_call" | custom-call | tf_op jit(solution)/shard_map/split/pallas_call | solution.py:68
  2.6 5.2 %collective-permute-start = (bf16[3,48,4096]{2,1,0:T(8,128)(2,1)S(1)}, bf16[3,48,4096]{2,1,0:T(8,128)(2,1)S(1)}, u32[]{:S(2)}, u32[]{:S(2)}) collective-permute-start(bf16[3,48,4096]{2,1,0:T(8,128)(2,1)S(1)} %get-tuple-element.18.far_ref), channel_id=1, source_target_pairs={{4,8},{8,4},{12,16},{16,12},{20,24},{24,20},{28,32},{32,28},{36,40... | collective-permute-start | bytes 3538952 | tf_op jit(solution)/shard_map/ppermute | solution.py:342
  7.8 1.4 %collective-permute-start.1 = (bf16[2,3,2,48,128]{4,3,2,1,0:T(8,128)(2,1)S(1)}, bf16[2,3,2,48,128]{4,3,2,1,0:T(8,128)(2,1)S(1)}, u32[]{:S(2)}, u32[]{:S(2)}) collective-permute-start(bf16[2,3,2,48,128]{4,3,2,1,0:T(8,128)(2,1)S(1)} %get-tuple-element.22.own_ref), channel_id=1, source_target_pairs={{0,1},{1,2},{2,3},{3,0},{4,5},{5,6},{6,7},{7,4},{8,9},{9,10},{10,1... | collective-permute-start | bytes 442376 | tf_op jit(solution)/shard_map/ppermute | solution.py:347
  9.2 2.6 %collective-permute-start.2 = (bf16[2,3,2,48,128]{4,3,2,1,0:T(8,128)(2,1)S(1)}, bf16[2,3,2,48,128]{4,3,2,1,0:T(8,128)(2,1)S(1)}, u32[]{:S(2)}, u32[]{:S(2)}) collective-permute-start(bf16[2,3,2,48,128]{4,3,2,1,0:T(8,128)(2,1)S(1)} %get-tuple-element.22.own_ref), channel_id=1, source_target_pairs={{0,2},{1,3},{2,0},{3,1},{4,6},{5,7},{6,4},{7,5},{8,10},{9,11},{10,... | collective-permute-start | bytes 442376 | tf_op jit(solution)/shard_map/ppermute | solution.py:347
  11.8 1.1 %collective-permute-start.3 = (bf16[2,3,2,48,128]{4,3,2,1,0:T(8,128)(2,1)S(1)}, bf16[2,3,2,48,128]{4,3,2,1,0:T(8,128)(2,1)S(1)}, u32[]{:S(2)}, u32[]{:S(2)}) collective-permute-start(bf16[2,3,2,48,128]{4,3,2,1,0:T(8,128)(2,1)S(1)} %get-tuple-element.22.own_ref), channel_id=1, source_target_pairs={{0,3},{1,0},{2,1},{3,2},{4,7},{5,4},{6,5},{7,6},{8,11},{9,8},{10,9... | collective-permute-start | bytes 442376 | tf_op jit(solution)/shard_map/ppermute | solution.py:347
  12.9 0.0 copy-done
  12.9 0.0 copy-start.1
  12.9 0.0 copy-start.2
  12.9 0.0 copy-start.3
  12.9 0.0 copy-start.4
  12.9 0.0 copy-start.5
  12.9 3.5 %bulk.1 = (f32[2,3,48,4096]{3,2,1,0:T(8,128)S(1)}, f32[3,48,128]{2,1,0:T(8,128)S(1)}) custom-call(bf16[48,432]{1,0:T(8,128)(2,1)S(1)} %copy-done, bf16[3,48,4096]{2,1,0:T(8,128)(2,1)S(1)} %get-tuple-element.19.near_ref, bf16[3,48,4096]{2,1,0:T(8,128)(2,1)S(1)} %get-tuple-element.18.far_ref), custom_call_target="tpu_custom_call" | custom-call | flops 5000000000 | bytes 5000000 | tf_op jit(solution)/shard_map/bulk/pallas_call | solution.py:162
  16.4 0.0 collective-permute-done.1.one_ref
  16.4 0.7 %collective-permute-done.2.two_ref = bf16[2,3,2,48,128]{4,3,2,1,0:T(8,128)(2,1)S(1)} collective-permute-done((bf16[2,3,2,48,128]{4,3,2,1,0:T(8,128)(2,1)S(1)}, bf16[2,3,2,48,128]{4,3,2,1,0:T(8,128)(2,1)S(1)}, u32[]{:S(2)}, u32[]{:S(2)}) %collective-permute-start.2) | collective-permute-done | bytes 147488 | tf_op jit(solution)/shard_map/ppermute | solution.py:347
  17.2 0.1 collective-permute-done.3.three_ref
  17.3 0.0 copy-done.1
  17.3 0.0 copy-done.2
  17.3 0.0 copy-done.3
  17.3 0.0 copy-done.4
  17.3 0.0 copy-done.5
  17.3 0.0 copy-start.6
  17.3 3.8 %own.1 = (bf16[3,48,4096]{2,1,0:T(8,128)(2,1)S(1)}, bf16[3,48,4096]{2,1,0:T(8,128)(2,1)S(1)}, bf16[9,48,128]{2,1,0:T(8,128)(2,1)S(1)}) custom-call(s32[1]{0:T(128)} %bitcast.1.me_ref, s32[1,3]{1,0:T(1,128)S(1)} %copy-done.1, s32[2,2,1,3]{3,2,1,0:T(1,128)S(1)} %bitcast.6, s32[2,2,3]{2,1,0:T(2,128)S(1)} %bitcast.7, bf16[48,432]{1,0:T(8,128)(2,1)S(1)} %copy-done, ...), custom_call_target="tpu_custom_call" | custom-call | tf_op jit(solution)/shard_map/own/pallas_call | solution.py:233
  21.1 0.1 collective-permute-start.5
  21.2 5.7 %collective-permute-start.4 = (bf16[9,48,128]{2,1,0:T(8,128)(2,1)S(1)}, bf16[9,48,128]{2,1,0:T(8,128)(2,1)S(1)}, u32[]{:S(2)}, u32[]{:S(2)}) collective-permute-start(bf16[9,48,128]{2,1,0:T(8,128)(2,1)S(1)} %get-tuple-element.28), channel_id=1, source_target_pairs={{4,8},{8,4},{12,16},{16,12},{20,24},{24,20},{28,32},{32,28},{36,40... | collective-permute-start | bytes 331784 | tf_op jit(solution)/shard_map/ppermute | solution.py:342
  26.9 0.0 collective-permute-done.raw_ref
  26.9 0.0 copy-done.6
  26.9 3.5 %inner.1 = (f32[3,48,4096]{2,1,0:T(8,128)S(1)}, f32[3,96,4096]{2,1,0:T(8,128)S(1)}, bf16[96,96]{1,0:T(8,128)(2,1)S(1)}) custom-call(s32[1]{0:T(128)} %bitcast.side_ref, bf16[48,432]{1,0:T(8,128)(2,1)S(1)} %copy-done, bf16[48,144]{1,0:T(8,128)(2,1)S(1)} %copy-done.6, bf16[3,48,2,4096]{3,2,1,0:T(2,128)(2,1)S(1)} %get-tuple-element.17.kept_ref, ...), custom_call_target="tpu_custom_call" | custom-call | flops 99999997952 | bytes 100000000 | tf_op jit(solution)/shard_map/inner/pallas_call | solution.py:283
  30.5 0.2 collective-permute-done.4.note_ref
  30.6 0.0 collective-permute-done.5.near_in_ref
  30.6 3.6 %final.1 = bf16[1,3,48,2,4096]{4,3,2,1,0:T(2,128)(2,1)} custom-call(s32[1,3]{1,0:T(1,128)S(1)} %copy-done.1, bf16[48,432]{1,0:T(8,128)(2,1)S(1)} %copy-done, bf16[96,96]{1,0:T(8,128)(2,1)S(1)} %get-tuple-element.25.matrix_ref, f32[3,48,4096]{2,1,0:T(8,128)S(1)} %get-tuple-element.26.plane_ref, f32[3,96,4096]{2,1,0:T(8,128)S(1)} %get-tuple-element.27.part_ref, ...), custom_call_target="tpu_custom_call" | custom-call | flops 2000000000 | bytes 2000000 | tf_op jit(solution)/shard_map/final/pallas_call | solution.py:327
Async XLA Ops:
  0.0 12.9 %copy-start = (bf16[48,432]{1,0:T(8,128)(2,1)S(1)}, bf16[48,432]{1,0:T(8,128)(2,1)}, u32[]{:S(2)}) copy-start(bf16[48,432]{1,0:T(8,128)(2,1)} %weight_ref.7) | copy-start | bytes 124420
  2.6 24.3 %collective-permute-start = (bf16[3,48,4096]{2,1,0:T(8,128)(2,1)S(1)}, bf16[3,48,4096]{2,1,0:T(8,128)(2,1)S(1)}, u32[]{:S(2)}, u32[]{:S(2)}) collective-permute-start(bf16[3,48,4096]{2,1,0:T(8,128)(2,1)S(1)} %get-tuple-element.18.far_ref), channel_id=1, source_target_pairs={{4,8},{8,4},{12,16},{16,12},{20,24},{24,20},{28,32},{32,28},{36,40... | collective-permute-start | bytes 3538952 | tf_op jit(solution)/shard_map/ppermute | solution.py:342
  7.8 8.6 %collective-permute-start.1 = (bf16[2,3,2,48,128]{4,3,2,1,0:T(8,128)(2,1)S(1)}, bf16[2,3,2,48,128]{4,3,2,1,0:T(8,128)(2,1)S(1)}, u32[]{:S(2)}, u32[]{:S(2)}) collective-permute-start(bf16[2,3,2,48,128]{4,3,2,1,0:T(8,128)(2,1)S(1)} %get-tuple-element.22.own_ref), channel_id=1, source_target_pairs={{0,1},{1,2},{2,3},{3,0},{4,5},{5,6},{6,7},{7,4},{8,9},{9,10},{10,1... | collective-permute-start | bytes 442376 | tf_op jit(solution)/shard_map/ppermute | solution.py:347
  9.2 8.0 %collective-permute-start.2 = (bf16[2,3,2,48,128]{4,3,2,1,0:T(8,128)(2,1)S(1)}, bf16[2,3,2,48,128]{4,3,2,1,0:T(8,128)(2,1)S(1)}, u32[]{:S(2)}, u32[]{:S(2)}) collective-permute-start(bf16[2,3,2,48,128]{4,3,2,1,0:T(8,128)(2,1)S(1)} %get-tuple-element.22.own_ref), channel_id=1, source_target_pairs={{0,2},{1,3},{2,0},{3,1},{4,6},{5,7},{6,4},{7,5},{8,10},{9,11},{10,... | collective-permute-start | bytes 442376 | tf_op jit(solution)/shard_map/ppermute | solution.py:347
  11.8 5.5 %collective-permute-start.3 = (bf16[2,3,2,48,128]{4,3,2,1,0:T(8,128)(2,1)S(1)}, bf16[2,3,2,48,128]{4,3,2,1,0:T(8,128)(2,1)S(1)}, u32[]{:S(2)}, u32[]{:S(2)}) collective-permute-start(bf16[2,3,2,48,128]{4,3,2,1,0:T(8,128)(2,1)S(1)} %get-tuple-element.22.own_ref), channel_id=1, source_target_pairs={{0,3},{1,0},{2,1},{3,2},{4,7},{5,4},{6,5},{7,6},{8,11},{9,8},{10,9... | collective-permute-start | bytes 442376 | tf_op jit(solution)/shard_map/ppermute | solution.py:347
  12.9 4.4 %copy-start.1 = (s32[1,3]{1,0:T(1,128)S(1)}, s32[1,3]{1,0:T(1,128)}, u32[]{:S(2)}) copy-start(s32[1,3]{1,0:T(1,128)} %live_ref.5) | copy-start | bytes 40
  12.9 4.4 %copy-start.2 = (s32[2,3,2,1]{1,3,2,0:T(1,128)S(1)}, s32[2,3,2,1]{1,3,2,0:T(1,128)}, u32[]{:S(2)}) copy-start(s32[2,3,2,1]{1,3,2,0:T(1,128)} %param.10) | copy-start | bytes 148
  12.9 4.4 %copy-start.3 = (s32[2,3,2]{1,2,0:T(2,128)S(1)}, s32[2,3,2]{1,2,0:T(2,128)}, u32[]{:S(2)}) copy-start(s32[2,3,2]{1,2,0:T(2,128)} %param.11) | copy-start | bytes 148
  12.9 4.4 %copy-start.4 = (f32[48]{0:T(128)S(1)}, f32[48]{0:T(128)}, u32[]{:S(2)}) copy-start(f32[48]{0:T(128)} %param.14) | copy-start | bytes 580
  12.9 4.4 %copy-start.5 = (f32[48]{0:T(128)S(1)}, f32[48]{0:T(128)}, u32[]{:S(2)}) copy-start(f32[48]{0:T(128)} %param.15) | copy-start | bytes 580
  17.3 9.6 %copy-start.6 = (bf16[48,144]{1,0:T(8,128)(2,1)S(1)}, bf16[48,144]{1,0:T(8,128)(2,1)}, u32[]{:S(2)}) copy-start(bf16[48,144]{1,0:T(8,128)(2,1)} %depth_ref.1) | copy-start | bytes 41476
  21.1 9.5 %collective-permute-start.5 = (bf16[3,48,4096]{2,1,0:T(8,128)(2,1)S(1)}, bf16[3,48,4096]{2,1,0:T(8,128)(2,1)S(1)}, u32[]{:S(2)}, u32[]{:S(2)}) collective-permute-start(bf16[3,48,4096]{2,1,0:T(8,128)(2,1)S(1)} %get-tuple-element.23.near_ref), channel_id=1, source_target_pairs={{0,4},{4,0},{8,12},{12,8},{16,20},{20,16},{24,28},{28,24},{32,36},... | collective-permute-start | bytes 3538952 | tf_op jit(solution)/shard_map/ppermute | solution.py:342
  21.2 9.4 %collective-permute-start.4 = (bf16[9,48,128]{2,1,0:T(8,128)(2,1)S(1)}, bf16[9,48,128]{2,1,0:T(8,128)(2,1)S(1)}, u32[]{:S(2)}, u32[]{:S(2)}) collective-permute-start(bf16[9,48,128]{2,1,0:T(8,128)(2,1)S(1)} %get-tuple-element.28), channel_id=1, source_target_pairs={{4,8},{8,4},{12,16},{16,12},{20,24},{24,20},{28,32},{32,28},{36,40... | collective-permute-start | bytes 331784 | tf_op jit(solution)/shard_map/ppermute | solution.py:342

commit v2 on v1

--- a/solution.py
+++ b/solution.py
@@ -43,6 +43,8 @@
     j = lax.broadcasted_iota(jnp.int32, (2 * c, 2 * c), 1)
     order = jnp.where(j == jnp.where(i < c, 2 * i + 1 - side, 2 * (i - c) + side), 1.0, 0.0).astype(BF)
     lane = lane_ids(2 * c)
+    edge = (lane + 1) % 64 < 2
+    zero = jnp.zeros((2 * c, LANES), BF)
     lives.wait()
     for b in range(SLOTS):
         copies[b].wait()
@@ -52,10 +54,10 @@
         far_ref[b] = d[c:]
         live = jnp.where(live_s[0, b] > 0, 1.0, 0.0).astype(BF)
         rows = jnp.where(lane < 64, d[:, :LANES], d[:, n - LANES:])
-        cols = jnp.zeros((2 * c, LANES), BF)
+        cols = zero
         for t in range(n // LANES):
-            tile = d[:, t * LANES:(t + 1) * LANES]
-            cols = jnp.where(lane % 64 // 2 == t, roll(tile, 2 * t + 65), cols)
+            tile = jnp.where(edge, d[:, t * LANES:(t + 1) * LANES], zero)
+            cols += roll(tile, 2 * t + 65)
         rows = rows * live
         cols = cols * live
         for q in range(2):
@@ -77,21 +79,22 @@
 
 
 def conv_layer(x_at, weight, stack, emit):
-    c, n = weight.shape[0] // 3, stack.shape[1]
+    c, n = stack.shape[1:]
     tiles = n // LANES
     lane = lane_ids(c)
     zero = jnp.zeros((c, LANES), BF)
     low = lane < 64
     for t in range(tiles):
         at = slice(t * LANES, (t + 1) * LANES)
-        tile = x_at(t)
-        stack[0:c, at] = jnp.where(lane % 64 == 0, zero, roll(tile, 1))
-        stack[c:2 * c, at] = tile
-        stack[2 * c:, at] = jnp.where(lane % 64 == 63, zero, roll(tile, -1))
+        tile = x_at(at)
+        stack[0, :, at] = jnp.where(lane % 64 == 0, zero, roll(tile, 1))
+        stack[1, :, at] = jnp.where(lane % 64 == 63, zero, roll(tile, -1))
     above = jnp.zeros((c, LANES), F32)
     middle = turned = None
     for pair in range(tiles // 2):
-        u = jnp.dot(weight, stack[:, pair * 2 * LANES:(pair + 1) * 2 * LANES], preferred_element_type=F32)
+        at = slice(pair * 2 * LANES, (pair + 1) * 2 * LANES)
+        taps = jnp.concatenate([stack[0, :, at], x_at(at), stack[1, :, at]], axis=0)
+        u = jnp.dot(weight, taps, preferred_element_type=F32)
         for h in range(2):
             part = u[:, h * LANES:(h + 1) * LANES]
             turn = roll(above + part[2 * c:], 64)
@@ -144,17 +147,43 @@
     return jnp.sum(jnp.where(i == j, jnp.broadcast_to(row, (c, c)), 0.0), axis=1, keepdims=True)
 
 
-def bulk_kernel(weight_ref, near_ref, far_ref, plane_ref, sum_ref, stack):
+def bulk_kernel(weight_ref, near_ref, far_ref, plane_ref, found_ref, stack):
     c, n = near_ref.shape[1:]
+    tiles = n // LANES
     weight = tap_rows(weight_ref[...])
+    lane = lane_ids(c)
+    edge = (lane + 1) % 64 < 2
+    low = lane < 64
+    inside = 2 * (n - 4 * 64 + 4)
     for b in range(SLOTS):
         total = [jnp.zeros((c, LANES), F32)]
+        outer = jnp.zeros((c, LANES), F32)
         for q, ref in enumerate((near_ref, far_ref)):
             def emit(t, value):
                 plane_ref[q, b, :, t * LANES:(t + 1) * LANES] = value
                 total[0] += value
-            conv_layer(lambda t: ref[b, :, t * LANES:(t + 1) * LANES], weight, stack, emit)
-        sum_ref[b] = total[0]
+            conv_layer(lambda at: ref[b, :, at], weight, stack, emit)
+            strip = jnp.zeros((c, LANES), F32)
+            for t in range(tiles):
+                strip += roll(jnp.where(edge, plane_ref[q, b, :, t * LANES:(t + 1) * LANES], 0.0), 2 * t)
+            rows = jnp.where(low, plane_ref[q, b, :, :LANES], plane_ref[q, b, :, n - LANES:])
+            rows = jnp.where(edge, 0.0, rows)
+            found_ref[b, 2 + q] = strip
+            found_ref[b, 4 + q] = rows
+            outer += strip + rows
+        mean = jnp.sum(total[0] - outer, axis=1, keepdims=True) * (1.0 / inside)
+        mean = jnp.broadcast_to(mean, (c, LANES))
+        square = jnp.zeros((c, LANES), F32)
+        for q in range(2):
+            for t in range(tiles):
+                off = jnp.where(edge, 0.0, plane_ref[q, b, :, t * LANES:(t + 1) * LANES] - mean)
+                if t == 0:
+                    off = jnp.where(low, 0.0, off)
+                if t == tiles - 1:
+                    off = jnp.where(low, off, 0.0)
+                square += off * off
+        found_ref[b, 0] = square
+        found_ref[b, 1] = mean
 
 
 def bulk(weight, near, far):
@@ -162,34 +191,35 @@
     return pl.pallas_call(
         bulk_kernel, name="bulk",
         in_specs=[VM] * 3, out_specs=[VM] * 2,
-        out_shape=[jax.ShapeDtypeStruct((2, s, c, n), F32), jax.ShapeDtypeStruct((s, c, LANES), F32)],
-        scratch_shapes=[pltpu.VMEM((3 * c, n), BF)],
+        out_shape=[jax.ShapeDtypeStruct((2, s, c, n), F32), jax.ShapeDtypeStruct((s, 6, c, LANES), F32)],
+        scratch_shapes=[pltpu.VMEM((2, c, n), BF)],
         compiler_params=params(8), cost_estimate=cost(5),
     )(weight, near, far)
 
 
-def own_kernel(me_ref, live_ref, owner_ref, slot_ref, weight_ref, gain_ref, bias_ref, plane_ref, sum_ref,
-               own_ref, one_ref, two_ref, three_ref, near_act, far_act, note_ref, table, off, edge):
-    c, n = near_act.shape[1:]
-    tiles = n // LANES
+def stats_kernel(me_ref, live_ref, owner_ref, slot_ref, weight_ref, gain_ref, bias_ref, found_ref,
+                 own_ref, one_ref, three_ref, two_ref, note_ref, edge_ref, norm_ref, table):
+    c = own_ref.shape[3]
+    n = 2 * 64 * 64
     lane = lane_ids(c)
+    side = (lane + 1) % 64 < 2
     me = me_ref[0]
     for k, ref in enumerate((own_ref, one_ref, two_ref, three_ref)):
         table[k] = ref[...]
     weight = tap_rows(weight_ref[...])
     gain_col = column(gain_ref[...])
     bias_col = column(bias_ref[...])
-    scale = 1.0 / (2 * n)
     note = jnp.zeros((c, LANES), F32)
+    edges, sums = [], []
 
     def pick(t, b, e):
         return lax.rem(me - owner_ref[t, e, 0, b] + 4, 4), slot_ref[t, e, b]
 
-    means, squares = [], []
     for b in range(SLOTS):
         south, north, west, east = pick(0, b, 1), pick(0, b, 0), pick(1, b, 0), pick(1, b, 1)
-        total = sum_ref[b]
-        terms = []
+        total = jnp.zeros((c, LANES), F32)
+        square = found_ref[b, 0]
+        base = found_ref[b, 1]
         for q in range(2):
             rows = jnp.where(lane < 64, table[south[0], q, south[1], 0], table[north[0], q, north[1], 0])
             cols = jnp.where(lane % 2 == 0, table[west[0], q, west[1], 1],
@@ -197,47 +227,71 @@
             if q == 1:
                 note_ref[2 * b] = rows
                 note_ref[2 * b + 1] = cols
-            for k, term in enumerate(edge_terms(rows, cols, weight)):
-                edge[b, q, k] = term
-                total += term
-        means.append(jnp.broadcast_to(jnp.sum(total, axis=1, keepdims=True) * scale, (c, LANES)))
-    for b in range(SLOTS):
-        square = jnp.zeros((c, LANES), F32)
+            top, bottom, strip = edge_terms(rows, cols, weight)
+            edges.append((top, bottom, strip))
+            corner = (jnp.where((lane == 0) | (lane == 63), top, 0.0)
+                      + jnp.where((lane == 126) | (lane == 61), roll(bottom, 62), 0.0))
+            col_off = found_ref[b, 2 + q] + strip + corner - base
+            row_off = jnp.where(side, 0.0, found_ref[b, 4 + q] + top + bottom - base)
+            total += col_off + row_off
+            square += col_off * col_off + row_off * row_off
+        sums.append((base, jnp.sum(total, axis=1, keepdims=True), jnp.sum(square, axis=1, keepdims=True)))
+    for b, (base, total, square) in enumerate(sums):
+        shift = total * (1.0 / n)
+        var = square * (1.0 / n) - shift * shift
+        live = jnp.where(live_ref[0, b] > 0, 1.0, 0.0)
+        gain = lax.rsqrt(jnp.maximum(var, 0.0) + 1e-05) * gain_col * live
+        for k, value in enumerate((base + shift, jnp.broadcast_to(gain, (c, LANES)),
+                                   jnp.broadcast_to(bias_col * live, (c, LANES)))):
+            norm_ref[b, k] = value
+            note = jnp.where(lane == 3 * b + k, value, note)
+    for b in range(SLOTS):
         for q in range(2):
-            terms = [edge[b, q, k] for k in range(3)]
-            for t in range(tiles):
-                at = slice(t * LANES, (t + 1) * LANES)
-                value = with_edges(plane_ref[q, b, :, at], t, tiles, terms) - means[b]
-                off[b, q, :, at] = value
-                square += value * value
-        squares.append(square)
-    for b in range(SLOTS):
-        var = jnp.sum(squares[b], axis=1, keepdims=True) * scale
-        live = jnp.where(live_ref[0, b] > 0, 1.0, 0.0)
-        gain_b = jnp.broadcast_to(lax.rsqrt(var + 1e-05) * gain_col * live, (c, LANES))
-        bias_b = jnp.broadcast_to(bias_col * live, (c, LANES))
-        for q, out in enumerate((near_act, far_act)):
-            for t in range(tiles):
-                at = slice(t * LANES, (t + 1) * LANES)
-                out[b, :, at] = jnp.maximum(off[b, q, :, at] * gain_b + bias_b, 0.0).astype(BF)
-        for k, value in enumerate((means[b], gain_b, bias_b)):
-            note = jnp.where(lane == 3 * b + k, value, note)
+            for k, term in enumerate(edges[2 * b + q]):
+                edge_ref[b, q, k] = term
     for k in range(3):
         part = note.astype(BF)
         note_ref[2 * SLOTS + k] = part
         note = note - part.astype(F32)
 
 
-def own_layers(me, live, owner, slot, weight, gain, bias, plane, sums, strips):
+def stats(me, live, owner, slot, weight, gain, bias, found, strips):
+    s, _, c, _ = found.shape
+    return pl.pallas_call(
+        stats_kernel, name="stats",
+        in_specs=[SM] * 4 + [VM] * 8, out_specs=[VM] * 3,
+        out_shape=[jax.ShapeDtypeStruct((2 * s + 3, c, LANES), BF), jax.ShapeDtypeStruct((s, 2, 3, c, LANES), F32),
+                   jax.ShapeDtypeStruct((s, 3, c, LANES), F32)],
+        scratch_shapes=[pltpu.VMEM((4,) + strips[0].shape, BF)],
+        compiler_params=params(8), cost_estimate=cost(0),
+    )(me, live, owner, slot, weight, gain, bias, found, *strips)
+
+
+def activate(plane_ref, edge_ref, norm_ref, q, b, store):
+    tiles = plane_ref.shape[3] // LANES
+    mean, gain, bias = (norm_ref[b, k] for k in range(3))
+    terms = [edge_ref[b, q, k] for k in range(3)]
+    for t in range(tiles):
+        at = slice(t * LANES, (t + 1) * LANES)
+        value = with_edges(plane_ref[q, b, :, at], t, tiles, terms) - mean
+        store(at, jnp.maximum(value * gain + bias, 0.0).astype(BF))
+
+
+def near_kernel(plane_ref, edge_ref, norm_ref, near_ref):
+    for b in range(SLOTS):
+        def store(at, value):
+            near_ref[b, :, at] = value
+        activate(plane_ref, edge_ref, norm_ref, 0, b, store)
+
+
+def near_layer(plane, edge, norm):
     _, s, c, n = plane.shape
     return pl.pallas_call(
-        own_kernel, name="own",
-        in_specs=[SM] * 4 + [VM] * 9, out_specs=[VM] * 3,
-        out_shape=[jax.ShapeDtypeStruct((s, c, n), BF)] * 2 + [jax.ShapeDtypeStruct((2 * s + 3, c, LANES), BF)],
-        scratch_shapes=[pltpu.VMEM((4,) + strips[0].shape, BF), pltpu.VMEM((s, 2, c, n), F32),
-                        pltpu.VMEM((s, 2, 3, c, LANES), F32)],
-        compiler_params=params(12), cost_estimate=cost(0),
-    )(me, live, owner, slot, weight, gain, bias, plane, sums, *strips)
+        near_kernel, name="near",
+        in_specs=[VM] * 3, out_specs=VM,
+        out_shape=jax.ShapeDtypeStruct((s, c, n), BF),
+        compiler_params=params(4), cost_estimate=cost(0),
+    )(plane, edge, norm)
 
 
 def depth_matrix(side, depth):
@@ -257,37 +311,39 @@
     return total.astype(BF)
 
 
-def inner_kernel(side_ref, weight_ref, depth_ref, kept_ref, raw_ref, near_ref, far_ref, plane_ref, part_ref, matrix_ref,
-                 stack, taps):
+def inner_kernel(side_ref, weight_ref, depth_ref, kept_ref, raw_ref, near_ref, own_ref, edge_ref, norm_ref,
+                 plane_ref, part_ref, matrix_ref, act, stack):
     c, n = near_ref.shape[1:]
-    weight = tap_rows(weight_ref[...])
     depth = depth_matrix(side_ref[0], depth_ref[...])
     matrix_ref[...] = jnp.concatenate([depth[:, :c], depth[:, 3 * c:]], axis=1)
     mine = depth[:, c:3 * c]
+    weight = tap_rows(weight_ref[...])
     wide = 512
     for b in range(SLOTS):
-        stack[0:c] = near_ref[b]
-        stack[c:] = far_ref[b]
+        def store(at, value):
+            act[:, at] = value
+        activate(own_ref, edge_ref, norm_ref, 1, b, store)
         for w in range(n // wide):
             at = slice(w * wide, (w + 1) * wide)
-            part_ref[b, :, at] = (jnp.dot(mine, stack[:, at], preferred_element_type=F32)
+            both = jnp.concatenate([near_ref[b, :, at], act[:, at]], axis=0)
+            part_ref[b, :, at] = (jnp.dot(mine, both, preferred_element_type=F32)
                                   + kept_ref[b, :, :, at].reshape(2 * c, wide).astype(F32))
 
         def emit(t, value):
             plane_ref[b, :, t * LANES:(t + 1) * LANES] = value
-        conv_layer(lambda t: raw_ref[b, :, t * LANES:(t + 1) * LANES], weight, taps, emit)
-
-
-def inner(side, weight, depth, kept, raw, near, far):
+        conv_layer(lambda at: raw_ref[b, :, at], weight, stack, emit)
+
+
+def inner(side, weight, depth, kept, raw, near, plane, edge, norm):
     s, c, n = near.shape
     return pl.pallas_call(
         inner_kernel, name="inner",
-        in_specs=[SM] + [VM] * 6, out_specs=[VM] * 3,
+        in_specs=[SM] + [VM] * 8, out_specs=[VM] * 3,
         out_shape=[jax.ShapeDtypeStruct((s, c, n), F32), jax.ShapeDtypeStruct((s, 2 * c, n), F32),
                    jax.ShapeDtypeStruct((2 * c, 2 * c), BF)],
-        scratch_shapes=[pltpu.VMEM((2 * c, n), BF), pltpu.VMEM((3 * c, n), BF)],
+        scratch_shapes=[pltpu.VMEM((c, n), BF), pltpu.VMEM((2, c, n), BF)],
         compiler_params=params(8), cost_estimate=cost(100),
-    )(side, weight, depth, kept, raw, near, far)
+    )(side, weight, depth, kept, raw, near, plane, edge, norm)
 
 
 def final_kernel(live_ref, weight_ref, matrix_ref, plane_ref, part_ref, note_ref, near_in_ref, out_ref, stack, done, edge, norm, sems):
@@ -306,15 +362,15 @@
     for b in range(SLOTS):
         mean, gain, bias = (norm[b, k] for k in range(3))
         terms = [edge[b, k] for k in range(3)]
-        stack[0:c] = near_in_ref[b]
         for t in range(tiles):
             at = slice(t * LANES, (t + 1) * LANES)
             value = with_edges(plane_ref[b, :, at], t, tiles, terms) - mean
-            stack[c:, at] = jnp.maximum(value * gain + bias, 0.0).astype(BF)
+            stack[:, at] = jnp.maximum(value * gain + bias, 0.0).astype(BF)
         live = jnp.where(live_ref[0, b] > 0, 1.0, 0.0)
         for w in range(n // wide):
             at = slice(w * wide, (w + 1) * wide)
-            mixed = jnp.dot(matrix, stack[:, at], preferred_element_type=F32)
+            both = jnp.concatenate([near_in_ref[b, :, at], stack[:, at]], axis=0)
+            mixed = jnp.dot(matrix, both, preferred_element_type=F32)
             done[b, :, :, at] = ((part_ref[b, :, at] + mixed) * live).astype(BF).reshape(c, 2, wide)
         copies.append(pltpu.make_async_copy(done.at[b], out_ref.at[0, b], sems.at[b]))
         copies[-1].start()
@@ -328,7 +384,7 @@
         final_kernel, name="final",
         in_specs=[SM] + [VM] * 6, out_specs=HB,
         out_shape=jax.ShapeDtypeStruct((1, s, c, 2, n), BF),
-        scratch_shapes=[pltpu.VMEM((2 * c, n), BF), pltpu.VMEM((s, c, 2, n), BF),
+        scratch_shapes=[pltpu.VMEM((c, n), BF), pltpu.VMEM((s, c, 2, n), BF),
                         pltpu.VMEM((s, 3, c, LANES), F32), pltpu.VMEM((s, 3, c, LANES), F32), pltpu.SemaphoreType.DMA((SLOTS,))],
         compiler_params=params(12), cost_estimate=cost(2),
     )(live, weight, matrix, plane, part, note, near_in)
@@ -356,12 +412,14 @@
     side = (lax.axis_index("slab") % 2).reshape(1)
     near, far, strips, kept = split(side, me, volume, tissue)
     raw = swap(far, "slab", 1)
-    strips = [strips] + [ring(strips, "blk", k) for k in (1, 2, 3)]
-    plane, sums = bulk(plane_weight, near, far)
-    near_act, far_act, note = own_layers(me, tissue, owner, slot, plane_weight, gain, bias, plane, sums, strips)
+    one, three, two = (ring(strips, "blk", k) for k in (1, 3, 2))
+    strips = [strips, one, three, two]
+    plane, found = bulk(plane_weight, near, far)
+    note, edge, norm = stats(me, tissue, owner, slot, plane_weight, gain, bias, found, strips)
     note_in = swap(note, "slab", 1)
+    near_act = near_layer(plane, edge, norm)
     near_in = swap(near_act, "slab", 0)
-    far_plane, part, matrix = inner(side, plane_weight, depth_weight, kept, raw, near_act, far_act)
+    far_plane, part, matrix = inner(side, plane_weight, depth_weight, kept, raw, near_act, plane, edge, norm)
     return final(tissue, plane_weight, matrix, far_plane, part, note_in, near_in)
 
 

time: 34.7 us -> 32.8 us (0.945)
  starting transfers between devices: 16.1 us -> 14.5 us
  Pallas kernels: 16.9 us -> 17.7 us
  waiting for transfers between devices: 1.02 us -> 0.22 us
    pallas_call x1, Pallas kernels: 3.5 us -> 5.78 us  [bulk(): pl.pallas_call(bulk_kernel, name='bulk', in_specs=[VM] * 3, out_specs=[VM...]
    pallas_call x2 -> x3, Pallas kernels: 7.3 us -> 5.76 us  [the longest x1 3.68 us: inner(): pl.pallas_call(inner_kernel, name='inner', in_specs=[SM] + [VM] * 8, out_...]
    ppermute x3, starting transfers between devices: 11 us -> 10 us  [swap(): return lax.ppermute(value, axis, pairs)]
    ppermute x3, waiting for transfers between devices: 0.86 us -> 0.01 us  [ring(): lax.ppermute(value, axis, [(i, (i + steps) % count) for i in range(count)])]
    ppermute x3, starting transfers between devices: 5.06 us -> 4.45 us  [ring(): lax.ppermute(value, axis, [(i, (i + steps) % count) for i in range(count)])]
  transfers between devices with their start and end apart: 6 -> 6, of which waited for: 3 -> 1; matrix products, arithmetic and copies ran while one was open for 0% -> 0% of each run, Pallas kernels for 31% -> 35%
where the time goes in v2:
time: 32.8 us; the launch traced here: 32.7 us
  Pallas kernels  17.7 us (54%)
  starting transfers between devices  14.5 us (44%)
  between operations  0.33 us (1%)
    ppermute x3, starting transfers between devices, swap(): return lax.ppermute(value, axis, pairs)  10 us
    pallas_call x1, Pallas kernels, bulk(): pl.pallas_call(bulk_kernel, name='bulk', in_specs=[VM] * 3, out_specs=[VM...  5.78 us
    ppermute x3, starting transfers between devices, ring(): lax.ppermute(value, axis, [(i, (i + steps) % count) for i in range(count)])  4.45 us
    pallas_call x1, Pallas kernels, inner(): pl.pallas_call(inner_kernel, name='inner', in_specs=[SM] + [VM] * 8, out_...  3.68 us
    pallas_call x1, Pallas kernels, final(): pl.pallas_call(final_kernel, name='final', in_specs=[SM] + [VM] * 6, out_...  3.54 us
    pallas_call x1, Pallas kernels, split(): pl.pallas_call(split_kernel, name='split', in_specs=[SM, SM, HB, HB], out...  2.57 us
    pallas_call x1, Pallas kernels, stats(): pl.pallas_call(stats_kernel, name='stats', in_specs=[SM] * 4 + [VM] * 8,...  1.41 us
    pallas_call x1, Pallas kernels, near_layer(): pl.pallas_call(near_kernel, name='near', in_specs=[VM] * 3, out_specs=VM,...  0.67 us
  transfers between devices with their start and end apart: 6, of which 1 were waited for; matrix products, arithmetic and copies ran while one was open for 0% of the time, Pallas kernels for 35%

profile of v2, /device:TPU:103, one launch (start us, length us, event | category | flops | bytes accessed | tf_op | source)
XLA Modules:
  0.0 32.7 jit_solution(8000133456030101404)
XLA Ops:
  0.0 0.0 copy-start
  0.0 2.6 %split.1 = (bf16[3,48,4096]{2,1,0:T(8,128)(2,1)S(1)}, bf16[3,48,4096]{2,1,0:T(8,128)(2,1)S(1)}, bf16[2,3,2,48,128]{4,3,2,1,0:T(8,128)(2,1)S(1)}, bf16[3,48,2,4096]{3,2,1,0:T(2,128)(2,1)S(1)}) custom-call(s32[1]{0:T(128)} %bitcast.side_ref, s32[1]{0:T(128)} %bitcast.1.me_ref, bf16[1,3,48,2,4096]{4,3,2,1,0:T(2,128)(2,1)} %vol_ref.1, s32[1,3]{1,0:T(1,128)} %live_ref.5), custom_call_target="tpu_custom_call" | custom-call | tf_op jit(solution)/shard_map/split/pallas_call | solution.py:70
  2.6 5.2 %collective-permute-start = (bf16[3,48,4096]{2,1,0:T(8,128)(2,1)S(1)}, bf16[3,48,4096]{2,1,0:T(8,128)(2,1)S(1)}, u32[]{:S(2)}, u32[]{:S(2)}) collective-permute-start(bf16[3,48,4096]{2,1,0:T(8,128)(2,1)S(1)} %get-tuple-element.18.far_ref), channel_id=1, source_target_pairs={{4,8},{8,4},{12,16},{16,12},{20,24},{24,20},{28,32},{32,28},{36,40... | collective-permute-start | bytes 3538952 | tf_op jit(solution)/shard_map/ppermute | solution.py:398
  7.8 3.0 %collective-permute-start.3 = (bf16[2,3,2,48,128]{4,3,2,1,0:T(8,128)(2,1)S(1)}, bf16[2,3,2,48,128]{4,3,2,1,0:T(8,128)(2,1)S(1)}, u32[]{:S(2)}, u32[]{:S(2)}) collective-permute-start(bf16[2,3,2,48,128]{4,3,2,1,0:T(8,128)(2,1)S(1)} %get-tuple-element.22.own_ref), channel_id=1, source_target_pairs={{0,2},{1,3},{2,0},{3,1},{4,6},{5,7},{6,4},{7,5},{8,10},{9,11},{10,... | collective-permute-start | bytes 442376 | tf_op jit(solution)/shard_map/ppermute | solution.py:403
  10.8 0.8 %collective-permute-start.2 = (bf16[2,3,2,48,128]{4,3,2,1,0:T(8,128)(2,1)S(1)}, bf16[2,3,2,48,128]{4,3,2,1,0:T(8,128)(2,1)S(1)}, u32[]{:S(2)}, u32[]{:S(2)}) collective-permute-start(bf16[2,3,2,48,128]{4,3,2,1,0:T(8,128)(2,1)S(1)} %get-tuple-element.22.own_ref), channel_id=1, source_target_pairs={{0,3},{1,0},{2,1},{3,2},{4,7},{5,4},{6,5},{7,6},{8,11},{9,8},{10,9... | collective-permute-start | bytes 442376 | tf_op jit(solution)/shard_map/ppermute | solution.py:403
  11.6 0.7 %collective-permute-start.1 = (bf16[2,3,2,48,128]{4,3,2,1,0:T(8,128)(2,1)S(1)}, bf16[2,3,2,48,128]{4,3,2,1,0:T(8,128)(2,1)S(1)}, u32[]{:S(2)}, u32[]{:S(2)}) collective-permute-start(bf16[2,3,2,48,128]{4,3,2,1,0:T(8,128)(2,1)S(1)} %get-tuple-element.22.own_ref), channel_id=1, source_target_pairs={{0,1},{1,2},{2,3},{3,0},{4,5},{5,6},{6,7},{7,4},{8,9},{9,10},{10,1... | collective-permute-start | bytes 442376 | tf_op jit(solution)/shard_map/ppermute | solution.py:403
  12.3 0.0 copy-done
  12.3 0.0 copy-start.1
  12.3 0.0 copy-start.2
  12.3 0.0 copy-start.3
  12.3 0.0 copy-start.4
  12.3 0.0 copy-start.5
  12.3 5.8 %bulk.1 = (f32[2,3,48,4096]{3,2,1,0:T(8,128)S(1)}, f32[3,6,48,128]{3,2,1,0:T(8,128)S(1)}) custom-call(bf16[48,432]{1,0:T(8,128)(2,1)S(1)} %copy-done, bf16[3,48,4096]{2,1,0:T(8,128)(2,1)S(1)} %get-tuple-element.19.near_ref, bf16[3,48,4096]{2,1,0:T(8,128)(2,1)S(1)} %get-tuple-element.18.far_ref), custom_call_target="tpu_custom_call" | custom-call | flops 5000000000 | bytes 5000000 | tf_op jit(solution)/shard_map/bulk/pallas_call | solution.py:191
  18.1 0.0 collective-permute-done.3.two_ref
  18.1 0.0 collective-permute-done.2.three_ref
  18.1 0.0 collective-permute-done.1.one_ref
  18.1 0.0 copy-done.1
  18.1 0.0 copy-done.2
  18.2 0.0 copy-done.3
  18.2 0.0 copy-done.4
  18.2 0.0 copy-done.5
  18.2 1.4 %stats.1 = (bf16[9,48,128]{2,1,0:T(8,128)(2,1)S(1)}, f32[3,2,3,48,128]{4,3,2,1,0:T(8,128)S(1)}, f32[3,3,48,128]{3,2,1,0:T(8,128)S(1)}) custom-call(s32[1]{0:T(128)} %bitcast.1.me_ref, s32[1,3]{1,0:T(1,128)S(1)} %copy-done.1, s32[2,2,1,3]{3,2,1,0:T(1,128)S(1)} %bitcast.6, s32[2,2,3]{2,1,0:T(2,128)S(1)} %bitcast.7, bf16[48,432]{1,0:T(8,128)(2,1)S(1)} %copy-done, ...), custom_call_target="tpu_custom_call" | custom-call | tf_op jit(solution)/shard_map/stats/pallas_call | solution.py:260
  19.6 4.5 %collective-permute-start.4 = (bf16[9,48,128]{2,1,0:T(8,128)(2,1)S(1)}, bf16[9,48,128]{2,1,0:T(8,128)(2,1)S(1)}, u32[]{:S(2)}, u32[]{:S(2)}) collective-permute-start(bf16[9,48,128]{2,1,0:T(8,128)(2,1)S(1)} %get-tuple-element.28), channel_id=1, source_target_pairs={{4,8},{8,4},{12,16},{16,12},{20,24},{24,20},{28,32},{32,28},{36,40... | collective-permute-start | bytes 331784 | tf_op jit(solution)/shard_map/ppermute | solution.py:398
  24.1 0.0 copy-start.6
  24.1 0.7 %near.1.near_ref = bf16[3,48,4096]{2,1,0:T(8,128)(2,1)S(1)} custom-call(f32[2,3,48,4096]{3,2,1,0:T(8,128)S(1)} %get-tuple-element.20.plane_ref.own_ref, f32[3,2,3,48,128]{4,3,2,1,0:T(8,128)S(1)} %get-tuple-element.23.edge_ref, f32[3,3,48,128]{3,2,1,0:T(8,128)S(1)} %get-tuple-element.24.norm_ref), custom_call_target="tpu_custom_call" | custom-call | tf_op jit(solution)/shard_map/near/pallas_call | solution.py:289
  24.8 0.3 collective-permute-start.5
  25.1 0.0 collective-permute-done.raw_ref
  25.1 0.0 copy-done.6
  25.1 3.7 %inner.1 = (f32[3,48,4096]{2,1,0:T(8,128)S(1)}, f32[3,96,4096]{2,1,0:T(8,128)S(1)}, bf16[96,96]{1,0:T(8,128)(2,1)S(1)}) custom-call(s32[1]{0:T(128)} %bitcast.side_ref, bf16[48,432]{1,0:T(8,128)(2,1)S(1)} %copy-done, bf16[48,144]{1,0:T(8,128)(2,1)S(1)} %copy-done.6, bf16[3,48,2,4096]{3,2,1,0:T(2,128)(2,1)S(1)} %get-tuple-element.17.kept_ref, ...), custom_call_target="tpu_custom_call" | custom-call | flops 99999997952 | bytes 100000000 | tf_op jit(solution)/shard_map/inner/pallas_call | solution.py:339
  28.8 0.2 collective-permute-done.4.note_ref
  29.0 0.0 collective-permute-done.5.near_in_ref
  29.0 3.5 %final.1 = bf16[1,3,48,2,4096]{4,3,2,1,0:T(2,128)(2,1)} custom-call(s32[1,3]{1,0:T(1,128)S(1)} %copy-done.1, bf16[48,432]{1,0:T(8,128)(2,1)S(1)} %copy-done, bf16[96,96]{1,0:T(8,128)(2,1)S(1)} %get-tuple-element.25.matrix_ref, f32[3,48,4096]{2,1,0:T(8,128)S(1)} %get-tuple-element.26.plane_ref, f32[3,96,4096]{2,1,0:T(8,128)S(1)} %get-tuple-element.27.part_ref, ...), custom_call_target="tpu_custom_call" | custom-call | flops 2000000000 | bytes 2000000 | tf_op jit(solution)/shard_map/final/pallas_call | solution.py:383
Async XLA Ops:
  0.0 12.3 %copy-start = (bf16[48,432]{1,0:T(8,128)(2,1)S(1)}, bf16[48,432]{1,0:T(8,128)(2,1)}, u32[]{:S(2)}) copy-start(bf16[48,432]{1,0:T(8,128)(2,1)} %weight_ref.7) | copy-start | bytes 124420
  2.6 22.5 %collective-permute-start = (bf16[3,48,4096]{2,1,0:T(8,128)(2,1)S(1)}, bf16[3,48,4096]{2,1,0:T(8,128)(2,1)S(1)}, u32[]{:S(2)}, u32[]{:S(2)}) collective-permute-start(bf16[3,48,4096]{2,1,0:T(8,128)(2,1)S(1)} %get-tuple-element.18.far_ref), channel_id=1, source_target_pairs={{4,8},{8,4},{12,16},{16,12},{20,24},{24,20},{28,32},{32,28},{36,40... | collective-permute-start | bytes 3538952 | tf_op jit(solution)/shard_map/ppermute | solution.py:398
  7.8 10.3 %collective-permute-start.3 = (bf16[2,3,2,48,128]{4,3,2,1,0:T(8,128)(2,1)S(1)}, bf16[2,3,2,48,128]{4,3,2,1,0:T(8,128)(2,1)S(1)}, u32[]{:S(2)}, u32[]{:S(2)}) collective-permute-start(bf16[2,3,2,48,128]{4,3,2,1,0:T(8,128)(2,1)S(1)} %get-tuple-element.22.own_ref), channel_id=1, source_target_pairs={{0,2},{1,3},{2,0},{3,1},{4,6},{5,7},{6,4},{7,5},{8,10},{9,11},{10,... | collective-permute-start | bytes 442376 | tf_op jit(solution)/shard_map/ppermute | solution.py:403
  10.8 7.3 %collective-permute-start.2 = (bf16[2,3,2,48,128]{4,3,2,1,0:T(8,128)(2,1)S(1)}, bf16[2,3,2,48,128]{4,3,2,1,0:T(8,128)(2,1)S(1)}, u32[]{:S(2)}, u32[]{:S(2)}) collective-permute-start(bf16[2,3,2,48,128]{4,3,2,1,0:T(8,128)(2,1)S(1)} %get-tuple-element.22.own_ref), channel_id=1, source_target_pairs={{0,3},{1,0},{2,1},{3,2},{4,7},{5,4},{6,5},{7,6},{8,11},{9,8},{10,9... | collective-permute-start | bytes 442376 | tf_op jit(solution)/shard_map/ppermute | solution.py:403
  11.6 6.5 %collective-permute-start.1 = (bf16[2,3,2,48,128]{4,3,2,1,0:T(8,128)(2,1)S(1)}, bf16[2,3,2,48,128]{4,3,2,1,0:T(8,128)(2,1)S(1)}, u32[]{:S(2)}, u32[]{:S(2)}) collective-permute-start(bf16[2,3,2,48,128]{4,3,2,1,0:T(8,128)(2,1)S(1)} %get-tuple-element.22.own_ref), channel_id=1, source_target_pairs={{0,1},{1,2},{2,3},{3,0},{4,5},{5,6},{6,7},{7,4},{8,9},{9,10},{10,1... | collective-permute-start | bytes 442376 | tf_op jit(solution)/shard_map/ppermute | solution.py:403
  12.3 5.9 %copy-start.1 = (s32[1,3]{1,0:T(1,128)S(1)}, s32[1,3]{1,0:T(1,128)}, u32[]{:S(2)}) copy-start(s32[1,3]{1,0:T(1,128)} %live_ref.5) | copy-start | bytes 40
  12.3 5.9 %copy-start.2 = (s32[2,3,2,1]{1,3,2,0:T(1,128)S(1)}, s32[2,3,2,1]{1,3,2,0:T(1,128)}, u32[]{:S(2)}) copy-start(s32[2,3,2,1]{1,3,2,0:T(1,128)} %param.10) | copy-start | bytes 148
  12.3 5.9 %copy-start.3 = (s32[2,3,2]{1,2,0:T(2,128)S(1)}, s32[2,3,2]{1,2,0:T(2,128)}, u32[]{:S(2)}) copy-start(s32[2,3,2]{1,2,0:T(2,128)} %param.11) | copy-start | bytes 148
  12.3 5.9 %copy-start.4 = (f32[48]{0:T(128)S(1)}, f32[48]{0:T(128)}, u32[]{:S(2)}) copy-start(f32[48]{0:T(128)} %param.14) | copy-start | bytes 580
  12.3 5.9 %copy-start.5 = (f32[48]{0:T(128)S(1)}, f32[48]{0:T(128)}, u32[]{:S(2)}) copy-start(f32[48]{0:T(128)} %param.15) | copy-start | bytes 580
  19.6 9.4 %collective-permute-start.4 = (bf16[9,48,128]{2,1,0:T(8,128)(2,1)S(1)}, bf16[9,48,128]{2,1,0:T(8,128)(2,1)S(1)}, u32[]{:S(2)}, u32[]{:S(2)}) collective-permute-start(bf16[9,48,128]{2,1,0:T(8,128)(2,1)S(1)} %get-tuple-element.28), channel_id=1, source_target_pairs={{4,8},{8,4},{12,16},{16,12},{20,24},{24,20},{28,32},{32,28},{36,40... | collective-permute-start | bytes 331784 | tf_op jit(solution)/shard_map/ppermute | solution.py:398
  24.1 1.0 %copy-start.6 = (bf16[48,144]{1,0:T(8,128)(2,1)S(1)}, bf16[48,144]{1,0:T(8,128)(2,1)}, u32[]{:S(2)}) copy-start(bf16[48,144]{1,0:T(8,128)(2,1)} %depth_ref.1) | copy-start | bytes 41476
  24.8 4.2 %collective-permute-start.5 = (bf16[3,48,4096]{2,1,0:T(8,128)(2,1)S(1)}, bf16[3,48,4096]{2,1,0:T(8,128)(2,1)S(1)}, u32[]{:S(2)}, u32[]{:S(2)}) collective-permute-start(bf16[3,48,4096]{2,1,0:T(8,128)(2,1)S(1)} %near.1.near_ref), channel_id=1, source_target_pairs={{0,4},{4,0},{8,12},{12,8},{16,20},{20,16},{24,28},{28,24},{32,36},... | collective-permute-start | bytes 3538952 | tf_op jit(solution)/shard_map/ppermute | solution.py:398

commit v3 on v2

--- a/solution.py
+++ b/solution.py
@@ -155,33 +155,35 @@
     edge = (lane + 1) % 64 < 2
     low = lane < 64
     inside = 2 * (n - 4 * 64 + 4)
+
+    def within(t, value):
+        if t == 0:
+            value = jnp.where(low, 0.0, value)
+        if t == tiles - 1:
+            value = jnp.where(low, value, 0.0)
+        return value
+
     for b in range(SLOTS):
         total = [jnp.zeros((c, LANES), F32)]
-        outer = jnp.zeros((c, LANES), F32)
         for q, ref in enumerate((near_ref, far_ref)):
             def emit(t, value):
                 plane_ref[q, b, :, t * LANES:(t + 1) * LANES] = value
-                total[0] += value
+                total[0] += within(t, jnp.where(edge, 0.0, value))
             conv_layer(lambda at: ref[b, :, at], weight, stack, emit)
-            strip = jnp.zeros((c, LANES), F32)
-            for t in range(tiles):
-                strip += roll(jnp.where(edge, plane_ref[q, b, :, t * LANES:(t + 1) * LANES], 0.0), 2 * t)
-            rows = jnp.where(low, plane_ref[q, b, :, :LANES], plane_ref[q, b, :, n - LANES:])
-            rows = jnp.where(edge, 0.0, rows)
-            found_ref[b, 2 + q] = strip
-            found_ref[b, 4 + q] = rows
-            outer += strip + rows
-        mean = jnp.sum(total[0] - outer, axis=1, keepdims=True) * (1.0 / inside)
+        mean = jnp.sum(total[0], axis=1, keepdims=True) * (1.0 / inside)
         mean = jnp.broadcast_to(mean, (c, LANES))
         square = jnp.zeros((c, LANES), F32)
         for q in range(2):
+            strip = jnp.zeros((c, LANES), F32)
             for t in range(tiles):
-                off = jnp.where(edge, 0.0, plane_ref[q, b, :, t * LANES:(t + 1) * LANES] - mean)
-                if t == 0:
-                    off = jnp.where(low, 0.0, off)
-                if t == tiles - 1:
-                    off = jnp.where(low, off, 0.0)
-                square += off * off
+                off = plane_ref[q, b, :, t * LANES:(t + 1) * LANES] - mean
+                side = jnp.where(edge, off, 0.0)
+                strip += roll(side, 2 * t)
+                inner = within(t, off - side)
+                square += inner * inner
+            rows = jnp.where(low, plane_ref[q, b, :, :LANES], plane_ref[q, b, :, n - LANES:]) - mean
+            found_ref[b, 2 + q] = strip
+            found_ref[b, 4 + q] = jnp.where(edge, 0.0, rows)
         found_ref[b, 0] = square
         found_ref[b, 1] = mean
 
@@ -231,8 +233,8 @@
             edges.append((top, bottom, strip))
             corner = (jnp.where((lane == 0) | (lane == 63), top, 0.0)
                       + jnp.where((lane == 126) | (lane == 61), roll(bottom, 62), 0.0))
-            col_off = found_ref[b, 2 + q] + strip + corner - base
-            row_off = jnp.where(side, 0.0, found_ref[b, 4 + q] + top + bottom - base)
+            col_off = found_ref[b, 2 + q] + strip + corner
+            row_off = jnp.where(side, 0.0, found_ref[b, 4 + q] + top + bottom)
             total += col_off + row_off
             square += col_off * col_off + row_off * row_off
         sums.append((base, jnp.sum(total, axis=1, keepdims=True), jnp.sum(square, axis=1, keepdims=True)))
@@ -249,10 +251,12 @@
         for q in range(2):
             for k, term in enumerate(edges[2 * b + q]):
                 edge_ref[b, q, k] = term
+    packed = jnp.zeros((c, LANES), F32)
     for k in range(3):
-        part = note.astype(BF)
-        note_ref[2 * SLOTS + k] = part
-        note = note - part.astype(F32)
+        part = note.astype(BF).astype(F32)
+        packed += roll(part, 3 * SLOTS * k)
+        note = note - part
+    note_ref[2 * SLOTS] = packed.astype(BF)
 
 
 def stats(me, live, owner, slot, weight, gain, bias, found, strips):
@@ -260,7 +264,7 @@
     return pl.pallas_call(
         stats_kernel, name="stats",
         in_specs=[SM] * 4 + [VM] * 8, out_specs=[VM] * 3,
-        out_shape=[jax.ShapeDtypeStruct((2 * s + 3, c, LANES), BF), jax.ShapeDtypeStruct((s, 2, 3, c, LANES), F32),
+        out_shape=[jax.ShapeDtypeStruct((2 * s + 1, c, LANES), BF), jax.ShapeDtypeStruct((s, 2, 3, c, LANES), F32),
                    jax.ShapeDtypeStruct((s, 3, c, LANES), F32)],
         scratch_shapes=[pltpu.VMEM((4,) + strips[0].shape, BF)],
         compiler_params=params(8), cost_estimate=cost(0),
@@ -351,7 +355,8 @@
     tiles = n // LANES
     weight = tap_rows(weight_ref[...])
     matrix = matrix_ref[...]
-    stats = note_ref[2 * SLOTS].astype(F32) + note_ref[2 * SLOTS + 1].astype(F32) + note_ref[2 * SLOTS + 2].astype(F32)
+    stats = note_ref[2 * SLOTS].astype(F32)
+    stats = stats + roll(stats, -3 * SLOTS) + roll(stats, -6 * SLOTS)
     wide = 512
     copies = []
     for b in range(SLOTS):
@@ -372,8 +377,11 @@
             both = jnp.concatenate([near_in_ref[b, :, at], stack[:, at]], axis=0)
             mixed = jnp.dot(matrix, both, preferred_element_type=F32)
             done[b, :, :, at] = ((part_ref[b, :, at] + mixed) * live).astype(BF).reshape(c, 2, wide)
-        copies.append(pltpu.make_async_copy(done.at[b], out_ref.at[0, b], sems.at[b]))
-        copies[-1].start()
+            if w % 2:
+                lanes = pl.ds((w - 1) * wide, 2 * wide)
+                copies.append(pltpu.make_async_copy(done.at[b, :, :, lanes], out_ref.at[0, b, :, :, lanes],
+                                                    sems.at[len(copies)]))
+                copies[-1].start()
     for copy in copies:
         copy.wait()
 
@@ -385,7 +393,8 @@
         in_specs=[SM] + [VM] * 6, out_specs=HB,
         out_shape=jax.ShapeDtypeStruct((1, s, c, 2, n), BF),
         scratch_shapes=[pltpu.VMEM((c, n), BF), pltpu.VMEM((s, c, 2, n), BF),
-                        pltpu.VMEM((s, 3, c, LANES), F32), pltpu.VMEM((s, 3, c, LANES), F32), pltpu.SemaphoreType.DMA((SLOTS,))],
+                        pltpu.VMEM((s, 3, c, LANES), F32), pltpu.VMEM((s, 3, c, LANES), F32),
+                        pltpu.SemaphoreType.DMA((n // 1024 * SLOTS,))],
         compiler_params=params(12), cost_estimate=cost(2),
     )(live, weight, matrix, plane, part, note, near_in)
 

time: 32.8 us -> 32.4 us (0.988)
  Pallas kernels: 17.7 us -> 17 us
  starting transfers between devices: 14.5 us -> 14.9 us
    pallas_call x1, Pallas kernels: 5.78 us -> 5.2 us  [bulk(): pl.pallas_call(bulk_kernel, name='bulk', in_specs=[VM] * 3, out_specs=[VM...]
    ppermute x3, starting transfers between devices: 10 us -> 10.4 us  [swap(): return lax.ppermute(value, axis, pairs)]
  transfers between devices with their start and end apart: 6 -> 6, of which waited for: 1 -> 0; matrix products, arithmetic and copies ran while one was open for 0% -> 0% of each run, Pallas kernels for 35% -> 34%
where the time goes in v3:
time: 32.4 us; the launch traced here: 32.3 us
  Pallas kernels  17 us (52%)
  starting transfers between devices  14.9 us (46%)
  between operations  0.34 us (1%)
    ppermute x3, starting transfers between devices, swap(): return lax.ppermute(value, axis, pairs)  10.4 us
    pallas_call x1, Pallas kernels, bulk(): pl.pallas_call(bulk_kernel, name='bulk', in_specs=[VM] * 3, out_specs=[VM...  5.2 us
    ppermute x3, starting transfers between devices, ring(): lax.ppermute(value, axis, [(i, (i + steps) % count) for i in range(count)])  4.45 us
    pallas_call x1, Pallas kernels, inner(): pl.pallas_call(inner_kernel, name='inner', in_specs=[SM] + [VM] * 8, out_...  3.71 us
    pallas_call x1, Pallas kernels, final(): pl.pallas_call(final_kernel, name='final', in_specs=[SM] + [VM] * 6, out_...  3.41 us
    pallas_call x1, Pallas kernels, split(): pl.pallas_call(split_kernel, name='split', in_specs=[SM, SM, HB, HB], out...  2.57 us
    pallas_call x1, Pallas kernels, stats(): pl.pallas_call(stats_kernel, name='stats', in_specs=[SM] * 4 + [VM] * 8,...  1.45 us
    pallas_call x1, Pallas kernels, near_layer(): pl.pallas_call(near_kernel, name='near', in_specs=[VM] * 3, out_specs=VM,...  0.69 us
  transfers between devices with their start and end apart: 6, of which 0 were waited for; matrix products, arithmetic and copies ran while one was open for 0% of the time, Pallas kernels for 34%

profile of v3, /device:TPU:103, one launch (start us, length us, event | category | flops | bytes accessed | tf_op | source)
XLA Modules:
  0.0 32.3 jit_solution(14753024485193590438)
XLA Ops:
  0.0 0.0 copy-start
  0.0 2.6 %split.1 = (bf16[3,48,4096]{2,1,0:T(8,128)(2,1)S(1)}, bf16[3,48,4096]{2,1,0:T(8,128)(2,1)S(1)}, bf16[2,3,2,48,128]{4,3,2,1,0:T(8,128)(2,1)S(1)}, bf16[3,48,2,4096]{3,2,1,0:T(2,128)(2,1)S(1)}) custom-call(s32[1]{0:T(128)} %bitcast.side_ref, s32[1]{0:T(128)} %bitcast.1.me_ref, bf16[1,3,48,2,4096]{4,3,2,1,0:T(2,128)(2,1)} %vol_ref.1, s32[1,3]{1,0:T(1,128)} %live_ref.5), custom_call_target="tpu_custom_call" | custom-call | tf_op jit(solution)/shard_map/split/pallas_call | solution.py:70
  2.6 5.2 %collective-permute-start = (bf16[3,48,4096]{2,1,0:T(8,128)(2,1)S(1)}, bf16[3,48,4096]{2,1,0:T(8,128)(2,1)S(1)}, u32[]{:S(2)}, u32[]{:S(2)}) collective-permute-start(bf16[3,48,4096]{2,1,0:T(8,128)(2,1)S(1)} %get-tuple-element.18.far_ref), channel_id=1, source_target_pairs={{4,8},{8,4},{12,16},{16,12},{20,24},{24,20},{28,32},{32,28},{36,40... | collective-permute-start | bytes 3538952 | tf_op jit(solution)/shard_map/ppermute | solution.py:407
  7.8 3.0 %collective-permute-start.3 = (bf16[2,3,2,48,128]{4,3,2,1,0:T(8,128)(2,1)S(1)}, bf16[2,3,2,48,128]{4,3,2,1,0:T(8,128)(2,1)S(1)}, u32[]{:S(2)}, u32[]{:S(2)}) collective-permute-start(bf16[2,3,2,48,128]{4,3,2,1,0:T(8,128)(2,1)S(1)} %get-tuple-element.22.own_ref), channel_id=1, source_target_pairs={{0,2},{1,3},{2,0},{3,1},{4,6},{5,7},{6,4},{7,5},{8,10},{9,11},{10,... | collective-permute-start | bytes 442376 | tf_op jit(solution)/shard_map/ppermute | solution.py:412
  10.8 0.8 %collective-permute-start.2 = (bf16[2,3,2,48,128]{4,3,2,1,0:T(8,128)(2,1)S(1)}, bf16[2,3,2,48,128]{4,3,2,1,0:T(8,128)(2,1)S(1)}, u32[]{:S(2)}, u32[]{:S(2)}) collective-permute-start(bf16[2,3,2,48,128]{4,3,2,1,0:T(8,128)(2,1)S(1)} %get-tuple-element.22.own_ref), channel_id=1, source_target_pairs={{0,3},{1,0},{2,1},{3,2},{4,7},{5,4},{6,5},{7,6},{8,11},{9,8},{10,9... | collective-permute-start | bytes 442376 | tf_op jit(solution)/shard_map/ppermute | solution.py:412
  11.6 0.7 %collective-permute-start.1 = (bf16[2,3,2,48,128]{4,3,2,1,0:T(8,128)(2,1)S(1)}, bf16[2,3,2,48,128]{4,3,2,1,0:T(8,128)(2,1)S(1)}, u32[]{:S(2)}, u32[]{:S(2)}) collective-permute-start(bf16[2,3,2,48,128]{4,3,2,1,0:T(8,128)(2,1)S(1)} %get-tuple-element.22.own_ref), channel_id=1, source_target_pairs={{0,1},{1,2},{2,3},{3,0},{4,5},{5,6},{6,7},{7,4},{8,9},{9,10},{10,1... | collective-permute-start | bytes 442376 | tf_op jit(solution)/shard_map/ppermute | solution.py:412
  12.3 0.0 copy-done
  12.3 0.0 copy-start.1
  12.3 0.0 copy-start.2
  12.3 0.0 copy-start.3
  12.3 0.0 copy-start.4
  12.3 0.0 copy-start.5
  12.3 5.2 %bulk.1 = (f32[2,3,48,4096]{3,2,1,0:T(8,128)S(1)}, f32[3,6,48,128]{3,2,1,0:T(8,128)S(1)}) custom-call(bf16[48,432]{1,0:T(8,128)(2,1)S(1)} %copy-done, bf16[3,48,4096]{2,1,0:T(8,128)(2,1)S(1)} %get-tuple-element.19.near_ref, bf16[3,48,4096]{2,1,0:T(8,128)(2,1)S(1)} %get-tuple-element.18.far_ref), custom_call_target="tpu_custom_call" | custom-call | flops 5000000000 | bytes 5000000 | tf_op jit(solution)/shard_map/bulk/pallas_call | solution.py:193
  17.5 0.0 collective-permute-done.3.two_ref
  17.5 0.0 collective-permute-done.2.three_ref
  17.5 0.0 collective-permute-done.1.one_ref
  17.6 0.0 copy-done.1
  17.6 0.0 copy-done.2
  17.6 0.0 copy-done.3
  17.6 0.0 copy-done.4
  17.6 0.0 copy-done.5
  17.6 1.4 %stats.1 = (bf16[7,48,128]{2,1,0:T(8,128)(2,1)S(1)}, f32[3,2,3,48,128]{4,3,2,1,0:T(8,128)S(1)}, f32[3,3,48,128]{3,2,1,0:T(8,128)S(1)}) custom-call(s32[1]{0:T(128)} %bitcast.1.me_ref, s32[1,3]{1,0:T(1,128)S(1)} %copy-done.1, s32[2,2,1,3]{3,2,1,0:T(1,128)S(1)} %bitcast.6, s32[2,2,3]{2,1,0:T(2,128)S(1)} %bitcast.7, bf16[48,432]{1,0:T(8,128)(2,1)S(1)} %copy-done, ...), custom_call_target="tpu_custom_call" | custom-call | tf_op jit(solution)/shard_map/stats/pallas_call | solution.py:264
  19.1 4.9 %collective-permute-start.4 = (bf16[7,48,128]{2,1,0:T(8,128)(2,1)S(1)}, bf16[7,48,128]{2,1,0:T(8,128)(2,1)S(1)}, u32[]{:S(2)}, u32[]{:S(2)}) collective-permute-start(bf16[7,48,128]{2,1,0:T(8,128)(2,1)S(1)} %get-tuple-element.28), channel_id=1, source_target_pairs={{4,8},{8,4},{12,16},{16,12},{20,24},{24,20},{28,32},{32,28},{36,40... | collective-permute-start | bytes 258056 | tf_op jit(solution)/shard_map/ppermute | solution.py:407
  24.0 0.0 copy-start.6
  24.0 0.7 %near.1.near_ref = bf16[3,48,4096]{2,1,0:T(8,128)(2,1)S(1)} custom-call(f32[2,3,48,4096]{3,2,1,0:T(8,128)S(1)} %get-tuple-element.20.plane_ref.own_ref, f32[3,2,3,48,128]{4,3,2,1,0:T(8,128)S(1)} %get-tuple-element.23.edge_ref, f32[3,3,48,128]{3,2,1,0:T(8,128)S(1)} %get-tuple-element.24.norm_ref), custom_call_target="tpu_custom_call" | custom-call | tf_op jit(solution)/shard_map/near/pallas_call | solution.py:293
  24.7 0.3 collective-permute-start.5
  24.9 0.0 collective-permute-done.raw_ref
  24.9 0.0 copy-done.6
  25.0 3.7 %inner.1 = (f32[3,48,4096]{2,1,0:T(8,128)S(1)}, f32[3,96,4096]{2,1,0:T(8,128)S(1)}, bf16[96,96]{1,0:T(8,128)(2,1)S(1)}) custom-call(s32[1]{0:T(128)} %bitcast.side_ref, bf16[48,432]{1,0:T(8,128)(2,1)S(1)} %copy-done, bf16[48,144]{1,0:T(8,128)(2,1)S(1)} %copy-done.6, bf16[3,48,2,4096]{3,2,1,0:T(2,128)(2,1)S(1)} %get-tuple-element.17.kept_ref, ...), custom_call_target="tpu_custom_call" | custom-call | flops 99999997952 | bytes 100000000 | tf_op jit(solution)/shard_map/inner/pallas_call | solution.py:343
  28.7 0.0 collective-permute-done.4.note_ref
  28.7 0.0 collective-permute-done.5.near_in_ref
  28.7 3.4 %final.1 = bf16[1,3,48,2,4096]{4,3,2,1,0:T(2,128)(2,1)} custom-call(s32[1,3]{1,0:T(1,128)S(1)} %copy-done.1, bf16[48,432]{1,0:T(8,128)(2,1)S(1)} %copy-done, bf16[96,96]{1,0:T(8,128)(2,1)S(1)} %get-tuple-element.25.matrix_ref, f32[3,48,4096]{2,1,0:T(8,128)S(1)} %get-tuple-element.26.plane_ref, f32[3,96,4096]{2,1,0:T(8,128)S(1)} %get-tuple-element.27.part_ref, ...), custom_call_target="tpu_custom_call" | custom-call | flops 2000000000 | bytes 2000000 | tf_op jit(solution)/shard_map/final/pallas_call | solution.py:391
Async XLA Ops:
  0.0 12.3 %copy-start = (bf16[48,432]{1,0:T(8,128)(2,1)S(1)}, bf16[48,432]{1,0:T(8,128)(2,1)}, u32[]{:S(2)}) copy-start(bf16[48,432]{1,0:T(8,128)(2,1)} %weight_ref.7) | copy-start | bytes 124420
  2.6 22.4 %collective-permute-start = (bf16[3,48,4096]{2,1,0:T(8,128)(2,1)S(1)}, bf16[3,48,4096]{2,1,0:T(8,128)(2,1)S(1)}, u32[]{:S(2)}, u32[]{:S(2)}) collective-permute-start(bf16[3,48,4096]{2,1,0:T(8,128)(2,1)S(1)} %get-tuple-element.18.far_ref), channel_id=1, source_target_pairs={{4,8},{8,4},{12,16},{16,12},{20,24},{24,20},{28,32},{32,28},{36,40... | collective-permute-start | bytes 3538952 | tf_op jit(solution)/shard_map/ppermute | solution.py:407
  7.8 9.7 %collective-permute-start.3 = (bf16[2,3,2,48,128]{4,3,2,1,0:T(8,128)(2,1)S(1)}, bf16[2,3,2,48,128]{4,3,2,1,0:T(8,128)(2,1)S(1)}, u32[]{:S(2)}, u32[]{:S(2)}) collective-permute-start(bf16[2,3,2,48,128]{4,3,2,1,0:T(8,128)(2,1)S(1)} %get-tuple-element.22.own_ref), channel_id=1, source_target_pairs={{0,2},{1,3},{2,0},{3,1},{4,6},{5,7},{6,4},{7,5},{8,10},{9,11},{10,... | collective-permute-start | bytes 442376 | tf_op jit(solution)/shard_map/ppermute | solution.py:412
  10.8 6.7 %collective-permute-start.2 = (bf16[2,3,2,48,128]{4,3,2,1,0:T(8,128)(2,1)S(1)}, bf16[2,3,2,48,128]{4,3,2,1,0:T(8,128)(2,1)S(1)}, u32[]{:S(2)}, u32[]{:S(2)}) collective-permute-start(bf16[2,3,2,48,128]{4,3,2,1,0:T(8,128)(2,1)S(1)} %get-tuple-element.22.own_ref), channel_id=1, source_target_pairs={{0,3},{1,0},{2,1},{3,2},{4,7},{5,4},{6,5},{7,6},{8,11},{9,8},{10,9... | collective-permute-start | bytes 442376 | tf_op jit(solution)/shard_map/ppermute | solution.py:412
  11.6 5.9 %collective-permute-start.1 = (bf16[2,3,2,48,128]{4,3,2,1,0:T(8,128)(2,1)S(1)}, bf16[2,3,2,48,128]{4,3,2,1,0:T(8,128)(2,1)S(1)}, u32[]{:S(2)}, u32[]{:S(2)}) collective-permute-start(bf16[2,3,2,48,128]{4,3,2,1,0:T(8,128)(2,1)S(1)} %get-tuple-element.22.own_ref), channel_id=1, source_target_pairs={{0,1},{1,2},{2,3},{3,0},{4,5},{5,6},{6,7},{7,4},{8,9},{9,10},{10,1... | collective-permute-start | bytes 442376 | tf_op jit(solution)/shard_map/ppermute | solution.py:412
  12.3 5.3 %copy-start.1 = (s32[1,3]{1,0:T(1,128)S(1)}, s32[1,3]{1,0:T(1,128)}, u32[]{:S(2)}) copy-start(s32[1,3]{1,0:T(1,128)} %live_ref.5) | copy-start | bytes 40
  12.3 5.3 %copy-start.2 = (s32[2,3,2,1]{1,3,2,0:T(1,128)S(1)}, s32[2,3,2,1]{1,3,2,0:T(1,128)}, u32[]{:S(2)}) copy-start(s32[2,3,2,1]{1,3,2,0:T(1,128)} %param.10) | copy-start | bytes 148
  12.3 5.3 %copy-start.3 = (s32[2,3,2]{1,2,0:T(2,128)S(1)}, s32[2,3,2]{1,2,0:T(2,128)}, u32[]{:S(2)}) copy-start(s32[2,3,2]{1,2,0:T(2,128)} %param.11) | copy-start | bytes 148
  12.3 5.3 %copy-start.4 = (f32[48]{0:T(128)S(1)}, f32[48]{0:T(128)}, u32[]{:S(2)}) copy-start(f32[48]{0:T(128)} %param.14) | copy-start | bytes 580
  12.3 5.3 %copy-start.5 = (f32[48]{0:T(128)S(1)}, f32[48]{0:T(128)}, u32[]{:S(2)}) copy-start(f32[48]{0:T(128)} %param.15) | copy-start | bytes 580
  19.1 9.6 %collective-permute-start.4 = (bf16[7,48,128]{2,1,0:T(8,128)(2,1)S(1)}, bf16[7,48,128]{2,1,0:T(8,128)(2,1)S(1)}, u32[]{:S(2)}, u32[]{:S(2)}) collective-permute-start(bf16[7,48,128]{2,1,0:T(8,128)(2,1)S(1)} %get-tuple-element.28), channel_id=1, source_target_pairs={{4,8},{8,4},{12,16},{16,12},{20,24},{24,20},{28,32},{32,28},{36,40... | collective-permute-start | bytes 258056 | tf_op jit(solution)/shard_map/ppermute | solution.py:407
  24.0 1.0 %copy-start.6 = (bf16[48,144]{1,0:T(8,128)(2,1)S(1)}, bf16[48,144]{1,0:T(8,128)(2,1)}, u32[]{:S(2)}) copy-start(bf16[48,144]{1,0:T(8,128)(2,1)} %depth_ref.1) | copy-start | bytes 41476
  24.7 4.0 %collective-permute-start.5 = (bf16[3,48,4096]{2,1,0:T(8,128)(2,1)S(1)}, bf16[3,48,4096]{2,1,0:T(8,128)(2,1)S(1)}, u32[]{:S(2)}, u32[]{:S(2)}) collective-permute-start(bf16[3,48,4096]{2,1,0:T(8,128)(2,1)S(1)} %near.1.near_ref), channel_id=1, source_target_pairs={{0,4},{4,0},{8,12},{12,8},{16,20},{20,16},{24,28},{28,24},{32,36},... | collective-permute-start | bytes 3538952 | tf_op jit(solution)/shard_map/ppermute | solution.py:407

commit v4 on v3

--- a/solution.py
+++ b/solution.py
@@ -147,10 +147,11 @@
     return jnp.sum(jnp.where(i == j, jnp.broadcast_to(row, (c, c)), 0.0), axis=1, keepdims=True)
 
 
-def bulk_kernel(weight_ref, near_ref, far_ref, plane_ref, found_ref, stack):
+def bulk_kernel(weight_ref, near_ref, far_ref, plane_ref, found_ref, taps_ref, stack):
     c, n = near_ref.shape[1:]
     tiles = n // LANES
     weight = tap_rows(weight_ref[...])
+    taps_ref[...] = weight
     lane = lane_ids(c)
     edge = (lane + 1) % 64 < 2
     low = lane < 64
@@ -192,8 +193,9 @@
     s, c, n = near.shape
     return pl.pallas_call(
         bulk_kernel, name="bulk",
-        in_specs=[VM] * 3, out_specs=[VM] * 2,
-        out_shape=[jax.ShapeDtypeStruct((2, s, c, n), F32), jax.ShapeDtypeStruct((s, 6, c, LANES), F32)],
+        in_specs=[VM] * 3, out_specs=[VM] * 3,
+        out_shape=[jax.ShapeDtypeStruct((2, s, c, n), F32), jax.ShapeDtypeStruct((s, 6, c, LANES), F32),
+                   jax.ShapeDtypeStruct((3 * c, 3 * c), BF)],
         scratch_shapes=[pltpu.VMEM((2, c, n), BF)],
         compiler_params=params(8), cost_estimate=cost(5),
     )(weight, near, far)
@@ -208,7 +210,7 @@
     me = me_ref[0]
     for k, ref in enumerate((own_ref, one_ref, two_ref, three_ref)):
         table[k] = ref[...]
-    weight = tap_rows(weight_ref[...])
+    weight = weight_ref[...]
     gain_col = column(gain_ref[...])
     bias_col = column(bias_ref[...])
     note = jnp.zeros((c, LANES), F32)
@@ -321,7 +323,7 @@
     depth = depth_matrix(side_ref[0], depth_ref[...])
     matrix_ref[...] = jnp.concatenate([depth[:, :c], depth[:, 3 * c:]], axis=1)
     mine = depth[:, c:3 * c]
-    weight = tap_rows(weight_ref[...])
+    weight = weight_ref[...]
     wide = 512
     for b in range(SLOTS):
         def store(at, value):
@@ -353,7 +355,7 @@
 def final_kernel(live_ref, weight_ref, matrix_ref, plane_ref, part_ref, note_ref, near_in_ref, out_ref, stack, done, edge, norm, sems):
     c, n = near_in_ref.shape[1:]
     tiles = n // LANES
-    weight = tap_rows(weight_ref[...])
+    weight = weight_ref[...]
     matrix = matrix_ref[...]
     stats = note_ref[2 * SLOTS].astype(F32)
     stats = stats + roll(stats, -3 * SLOTS) + roll(stats, -6 * SLOTS)
@@ -371,12 +373,12 @@
             at = slice(t * LANES, (t + 1) * LANES)
             value = with_edges(plane_ref[b, :, at], t, tiles, terms) - mean
             stack[:, at] = jnp.maximum(value * gain + bias, 0.0).astype(BF)
-        live = jnp.where(live_ref[0, b] > 0, 1.0, 0.0)
+        live = jnp.where(live_ref[0, b] > 0, 1.0, 0.0).astype(BF)
         for w in range(n // wide):
             at = slice(w * wide, (w + 1) * wide)
             both = jnp.concatenate([near_in_ref[b, :, at], stack[:, at]], axis=0)
             mixed = jnp.dot(matrix, both, preferred_element_type=F32)
-            done[b, :, :, at] = ((part_ref[b, :, at] + mixed) * live).astype(BF).reshape(c, 2, wide)
+            done[b, :, :, at] = ((part_ref[b, :, at] + mixed).astype(BF) * live).reshape(c, 2, wide)
             if w % 2:
                 lanes = pl.ds((w - 1) * wide, 2 * wide)
                 copies.append(pltpu.make_async_copy(done.at[b, :, :, lanes], out_ref.at[0, b, :, :, lanes],
@@ -423,13 +425,13 @@
     raw = swap(far, "slab", 1)
     one, three, two = (ring(strips, "blk", k) for k in (1, 3, 2))
     strips = [strips, one, three, two]
-    plane, found = bulk(plane_weight, near, far)
-    note, edge, norm = stats(me, tissue, owner, slot, plane_weight, gain, bias, found, strips)
+    plane, found, taps = bulk(plane_weight, near, far)
+    note, edge, norm = stats(me, tissue, owner, slot, taps, gain, bias, found, strips)
     note_in = swap(note, "slab", 1)
     near_act = near_layer(plane, edge, norm)
     near_in = swap(near_act, "slab", 0)
-    far_plane, part, matrix = inner(side, plane_weight, depth_weight, kept, raw, near_act, plane, edge, norm)
-    return final(tissue, plane_weight, matrix, far_plane, part, note_in, near_in)
+    far_plane, part, matrix = inner(side, taps, depth_weight, kept, raw, near_act, plane, edge, norm)
+    return final(tissue, taps, matrix, far_plane, part, note_in, near_in)
 
 
 def solution(mesh):

time: 32.4 us -> 32.5 us (level)
  no operation moved by 1% of the time
where the time goes in v4:
time: 32.5 us; the launch traced here: 32.4 us
  Pallas kernels  17.1 us (53%)
  starting transfers between devices  14.9 us (46%)
  between operations  0.34 us (1%)
    ppermute x3, starting transfers between devices, swap(): return lax.ppermute(value, axis, pairs)  10.4 us
    pallas_call x1, Pallas kernels, bulk(): pl.pallas_call(bulk_kernel, name='bulk', in_specs=[VM] * 3, out_specs=[VM...  5.18 us
    ppermute x3, starting transfers between devices, ring(): lax.ppermute(value, axis, [(i, (i + steps) % count) for i in range(count)])  4.43 us
    pallas_call x1, Pallas kernels, inner(): pl.pallas_call(inner_kernel, name='inner', in_specs=[SM] + [VM] * 8, out_...  3.76 us
    pallas_call x1, Pallas kernels, final(): pl.pallas_call(final_kernel, name='final', in_specs=[SM] + [VM] * 6, out_...  3.5 us
    pallas_call x1, Pallas kernels, split(): pl.pallas_call(split_kernel, name='split', in_specs=[SM, SM, HB, HB], out...  2.56 us
    pallas_call x1, Pallas kernels, stats(): pl.pallas_call(stats_kernel, name='stats', in_specs=[SM] * 4 + [VM] * 8,...  1.45 us
    pallas_call x1, Pallas kernels, near_layer(): pl.pallas_call(near_kernel, name='near', in_specs=[VM] * 3, out_specs=VM,...  0.68 us
  transfers between devices with their start and end apart: 6, of which 0 were waited for; matrix products, arithmetic and copies ran while one was open for 0% of the time, Pallas kernels for 34%

profile of v4, /device:TPU:103, one launch (start us, length us, event | category | flops | bytes accessed | tf_op | source)
XLA Modules:
  0.0 32.4 jit_solution(8574398611941417219)
XLA Ops:
  0.0 0.0 copy-start.5
  0.0 2.6 %split.1 = (bf16[3,48,4096]{2,1,0:T(8,128)(2,1)S(1)}, bf16[3,48,4096]{2,1,0:T(8,128)(2,1)S(1)}, bf16[2,3,2,48,128]{4,3,2,1,0:T(8,128)(2,1)S(1)}, bf16[3,48,2,4096]{3,2,1,0:T(2,128)(2,1)S(1)}) custom-call(s32[1]{0:T(128)} %bitcast.side_ref, s32[1]{0:T(128)} %bitcast.1.me_ref, bf16[1,3,48,2,4096]{4,3,2,1,0:T(2,128)(2,1)} %vol_ref.1, s32[1,3]{1,0:T(1,128)} %live_ref.5), custom_call_target="tpu_custom_call" | custom-call | tf_op jit(solution)/shard_map/split/pallas_call | solution.py:70
  2.6 5.3 %collective-permute-start = (bf16[3,48,4096]{2,1,0:T(8,128)(2,1)S(1)}, bf16[3,48,4096]{2,1,0:T(8,128)(2,1)S(1)}, u32[]{:S(2)}, u32[]{:S(2)}) collective-permute-start(bf16[3,48,4096]{2,1,0:T(8,128)(2,1)S(1)} %get-tuple-element.19.far_ref), channel_id=1, source_target_pairs={{4,8},{8,4},{12,16},{16,12},{20,24},{24,20},{28,32},{32,28},{36,40... | collective-permute-start | bytes 3538952 | tf_op jit(solution)/shard_map/ppermute | solution.py:409
  7.8 3.0 %collective-permute-start.3 = (bf16[2,3,2,48,128]{4,3,2,1,0:T(8,128)(2,1)S(1)}, bf16[2,3,2,48,128]{4,3,2,1,0:T(8,128)(2,1)S(1)}, u32[]{:S(2)}, u32[]{:S(2)}) collective-permute-start(bf16[2,3,2,48,128]{4,3,2,1,0:T(8,128)(2,1)S(1)} %get-tuple-element.24.own_ref), channel_id=1, source_target_pairs={{0,2},{1,3},{2,0},{3,1},{4,6},{5,7},{6,4},{7,5},{8,10},{9,11},{10,... | collective-permute-start | bytes 442376 | tf_op jit(solution)/shard_map/ppermute | solution.py:414
  10.8 0.8 %collective-permute-start.2 = (bf16[2,3,2,48,128]{4,3,2,1,0:T(8,128)(2,1)S(1)}, bf16[2,3,2,48,128]{4,3,2,1,0:T(8,128)(2,1)S(1)}, u32[]{:S(2)}, u32[]{:S(2)}) collective-permute-start(bf16[2,3,2,48,128]{4,3,2,1,0:T(8,128)(2,1)S(1)} %get-tuple-element.24.own_ref), channel_id=1, source_target_pairs={{0,3},{1,0},{2,1},{3,2},{4,7},{5,4},{6,5},{7,6},{8,11},{9,8},{10,9... | collective-permute-start | bytes 442376 | tf_op jit(solution)/shard_map/ppermute | solution.py:414
  11.6 0.7 %collective-permute-start.1 = (bf16[2,3,2,48,128]{4,3,2,1,0:T(8,128)(2,1)S(1)}, bf16[2,3,2,48,128]{4,3,2,1,0:T(8,128)(2,1)S(1)}, u32[]{:S(2)}, u32[]{:S(2)}) collective-permute-start(bf16[2,3,2,48,128]{4,3,2,1,0:T(8,128)(2,1)S(1)} %get-tuple-element.24.own_ref), channel_id=1, source_target_pairs={{0,1},{1,2},{2,3},{3,0},{4,5},{5,6},{6,7},{7,4},{8,9},{9,10},{10,1... | collective-permute-start | bytes 442376 | tf_op jit(solution)/shard_map/ppermute | solution.py:414
  12.3 0.0 copy-done.5
  12.3 0.0 copy-start
  12.3 0.0 copy-start.1
  12.3 0.0 copy-start.2
  12.3 0.0 copy-start.3
  12.3 0.0 copy-start.4
  12.3 5.2 %bulk.1 = (f32[2,3,48,4096]{3,2,1,0:T(8,128)S(1)}, f32[3,6,48,128]{3,2,1,0:T(8,128)S(1)}, bf16[144,144]{1,0:T(8,128)(2,1)S(1)}) custom-call(bf16[48,432]{1,0:T(8,128)(2,1)S(1)} %copy-done.5, bf16[3,48,4096]{2,1,0:T(8,128)(2,1)S(1)} %get-tuple-element.18.near_ref, bf16[3,48,4096]{2,1,0:T(8,128)(2,1)S(1)} %get-tuple-element.19.far_ref), custom_call_target="tpu_custom_call" | custom-call | flops 5000000000 | bytes 5000000 | tf_op jit(solution)/shard_map/bulk/pallas_call | solution.py:194
  17.5 0.0 collective-permute-done.3.two_ref
  17.5 0.0 collective-permute-done.2.three_ref
  17.5 0.0 collective-permute-done.1.one_ref
  17.5 0.0 copy-done
  17.5 0.0 copy-done.1
  17.6 0.0 copy-done.2
  17.6 0.0 copy-done.3
  17.6 0.0 copy-done.4
  17.6 1.4 %stats.1 = (bf16[7,48,128]{2,1,0:T(8,128)(2,1)S(1)}, f32[3,2,3,48,128]{4,3,2,1,0:T(8,128)S(1)}, f32[3,3,48,128]{3,2,1,0:T(8,128)S(1)}) custom-call(s32[1]{0:T(128)} %bitcast.1.me_ref, s32[1,3]{1,0:T(1,128)S(1)} %copy-done, s32[2,2,1,3]{3,2,1,0:T(1,128)S(1)} %bitcast.6, s32[2,2,3]{2,1,0:T(2,128)S(1)} %bitcast.7, ...), custom_call_target="tpu_custom_call" | custom-call | tf_op jit(solution)/shard_map/stats/pallas_call | solution.py:266
  19.0 4.9 %collective-permute-start.4 = (bf16[7,48,128]{2,1,0:T(8,128)(2,1)S(1)}, bf16[7,48,128]{2,1,0:T(8,128)(2,1)S(1)}, u32[]{:S(2)}, u32[]{:S(2)}) collective-permute-start(bf16[7,48,128]{2,1,0:T(8,128)(2,1)S(1)} %get-tuple-element.30), channel_id=1, source_target_pairs={{4,8},{8,4},{12,16},{16,12},{20,24},{24,20},{28,32},{32,28},{36,40... | collective-permute-start | bytes 258056 | tf_op jit(solution)/shard_map/ppermute | solution.py:409
  23.9 0.0 copy-start.6
  23.9 0.7 %near.1.near_ref = bf16[3,48,4096]{2,1,0:T(8,128)(2,1)S(1)} custom-call(f32[2,3,48,4096]{3,2,1,0:T(8,128)S(1)} %get-tuple-element.22.plane_ref.own_ref, f32[3,2,3,48,128]{4,3,2,1,0:T(8,128)S(1)} %get-tuple-element.25.edge_ref, f32[3,3,48,128]{3,2,1,0:T(8,128)S(1)} %get-tuple-element.26.norm_ref), custom_call_target="tpu_custom_call" | custom-call | tf_op jit(solution)/shard_map/near/pallas_call | solution.py:295
  24.6 0.3 collective-permute-start.5
  24.9 0.0 collective-permute-done.raw_ref
  24.9 0.0 copy-done.6
  24.9 3.8 %inner.1 = (f32[3,48,4096]{2,1,0:T(8,128)S(1)}, f32[3,96,4096]{2,1,0:T(8,128)S(1)}, bf16[96,96]{1,0:T(8,128)(2,1)S(1)}) custom-call(s32[1]{0:T(128)} %bitcast.side_ref, bf16[144,144]{1,0:T(8,128)(2,1)S(1)} %get-tuple-element.20.weight_ref, bf16[48,144]{1,0:T(8,128)(2,1)S(1)} %copy-done.6, bf16[3,48,2,4096]{3,2,1,0:T(2,128)(2,1)S(1)} %get-tuple-element.21.kept_ref, ...), custom_call_target="tpu_custom_call" | custom-call | flops 99999997952 | bytes 100000000 | tf_op jit(solution)/shard_map/inner/pallas_call | solution.py:345
  28.7 0.0 collective-permute-done.4.note_ref
  28.7 0.0 collective-permute-done.5.near_in_ref
  28.7 3.5 %final.1 = bf16[1,3,48,2,4096]{4,3,2,1,0:T(2,128)(2,1)} custom-call(s32[1,3]{1,0:T(1,128)S(1)} %copy-done, bf16[144,144]{1,0:T(8,128)(2,1)S(1)} %get-tuple-element.20.weight_ref, bf16[96,96]{1,0:T(8,128)(2,1)S(1)} %get-tuple-element.27.matrix_ref, f32[3,48,4096]{2,1,0:T(8,128)S(1)} %get-tuple-element.28.plane_ref, ...), custom_call_target="tpu_custom_call" | custom-call | flops 2000000000 | bytes 2000000 | tf_op jit(solution)/shard_map/final/pallas_call | solution.py:393
Async XLA Ops:
  0.0 12.3 %copy-start.5 = (bf16[48,432]{1,0:T(8,128)(2,1)S(1)}, bf16[48,432]{1,0:T(8,128)(2,1)}, u32[]{:S(2)}) copy-start(bf16[48,432]{1,0:T(8,128)(2,1)} %weight_ref.1) | copy-start | bytes 124420
  2.6 22.3 %collective-permute-start = (bf16[3,48,4096]{2,1,0:T(8,128)(2,1)S(1)}, bf16[3,48,4096]{2,1,0:T(8,128)(2,1)S(1)}, u32[]{:S(2)}, u32[]{:S(2)}) collective-permute-start(bf16[3,48,4096]{2,1,0:T(8,128)(2,1)S(1)} %get-tuple-element.19.far_ref), channel_id=1, source_target_pairs={{4,8},{8,4},{12,16},{16,12},{20,24},{24,20},{28,32},{32,28},{36,40... | collective-permute-start | bytes 3538952 | tf_op jit(solution)/shard_map/ppermute | solution.py:409
  7.8 9.7 %collective-permute-start.3 = (bf16[2,3,2,48,128]{4,3,2,1,0:T(8,128)(2,1)S(1)}, bf16[2,3,2,48,128]{4,3,2,1,0:T(8,128)(2,1)S(1)}, u32[]{:S(2)}, u32[]{:S(2)}) collective-permute-start(bf16[2,3,2,48,128]{4,3,2,1,0:T(8,128)(2,1)S(1)} %get-tuple-element.24.own_ref), channel_id=1, source_target_pairs={{0,2},{1,3},{2,0},{3,1},{4,6},{5,7},{6,4},{7,5},{8,10},{9,11},{10,... | collective-permute-start | bytes 442376 | tf_op jit(solution)/shard_map/ppermute | solution.py:414
  10.8 6.7 %collective-permute-start.2 = (bf16[2,3,2,48,128]{4,3,2,1,0:T(8,128)(2,1)S(1)}, bf16[2,3,2,48,128]{4,3,2,1,0:T(8,128)(2,1)S(1)}, u32[]{:S(2)}, u32[]{:S(2)}) collective-permute-start(bf16[2,3,2,48,128]{4,3,2,1,0:T(8,128)(2,1)S(1)} %get-tuple-element.24.own_ref), channel_id=1, source_target_pairs={{0,3},{1,0},{2,1},{3,2},{4,7},{5,4},{6,5},{7,6},{8,11},{9,8},{10,9... | collective-permute-start | bytes 442376 | tf_op jit(solution)/shard_map/ppermute | solution.py:414
  11.6 5.9 %collective-permute-start.1 = (bf16[2,3,2,48,128]{4,3,2,1,0:T(8,128)(2,1)S(1)}, bf16[2,3,2,48,128]{4,3,2,1,0:T(8,128)(2,1)S(1)}, u32[]{:S(2)}, u32[]{:S(2)}) collective-permute-start(bf16[2,3,2,48,128]{4,3,2,1,0:T(8,128)(2,1)S(1)} %get-tuple-element.24.own_ref), channel_id=1, source_target_pairs={{0,1},{1,2},{2,3},{3,0},{4,5},{5,6},{6,7},{7,4},{8,9},{9,10},{10,1... | collective-permute-start | bytes 442376 | tf_op jit(solution)/shard_map/ppermute | solution.py:414
  12.3 5.3 %copy-start = (s32[1,3]{1,0:T(1,128)S(1)}, s32[1,3]{1,0:T(1,128)}, u32[]{:S(2)}) copy-start(s32[1,3]{1,0:T(1,128)} %live_ref.5) | copy-start | bytes 40
  12.3 5.3 %copy-start.1 = (s32[2,3,2,1]{1,3,2,0:T(1,128)S(1)}, s32[2,3,2,1]{1,3,2,0:T(1,128)}, u32[]{:S(2)}) copy-start(s32[2,3,2,1]{1,3,2,0:T(1,128)} %param.10) | copy-start | bytes 148
  12.3 5.3 %copy-start.2 = (s32[2,3,2]{1,2,0:T(2,128)S(1)}, s32[2,3,2]{1,2,0:T(2,128)}, u32[]{:S(2)}) copy-start(s32[2,3,2]{1,2,0:T(2,128)} %param.11) | copy-start | bytes 148
  12.3 5.3 %copy-start.3 = (f32[48]{0:T(128)S(1)}, f32[48]{0:T(128)}, u32[]{:S(2)}) copy-start(f32[48]{0:T(128)} %param.14) | copy-start | bytes 580
  12.3 5.3 %copy-start.4 = (f32[48]{0:T(128)S(1)}, f32[48]{0:T(128)}, u32[]{:S(2)}) copy-start(f32[48]{0:T(128)} %param.15) | copy-start | bytes 580
  19.0 9.7 %collective-permute-start.4 = (bf16[7,48,128]{2,1,0:T(8,128)(2,1)S(1)}, bf16[7,48,128]{2,1,0:T(8,128)(2,1)S(1)}, u32[]{:S(2)}, u32[]{:S(2)}) collective-permute-start(bf16[7,48,128]{2,1,0:T(8,128)(2,1)S(1)} %get-tuple-element.30), channel_id=1, source_target_pairs={{4,8},{8,4},{12,16},{16,12},{20,24},{24,20},{28,32},{32,28},{36,40... | collective-permute-start | bytes 258056 | tf_op jit(solution)/shard_map/ppermute | solution.py:409
  23.9 1.0 %copy-start.6 = (bf16[48,144]{1,0:T(8,128)(2,1)S(1)}, bf16[48,144]{1,0:T(8,128)(2,1)}, u32[]{:S(2)}) copy-start(bf16[48,144]{1,0:T(8,128)(2,1)} %depth_ref.1) | copy-start | bytes 41476
  24.6 4.1 %collective-permute-start.5 = (bf16[3,48,4096]{2,1,0:T(8,128)(2,1)S(1)}, bf16[3,48,4096]{2,1,0:T(8,128)(2,1)S(1)}, u32[]{:S(2)}, u32[]{:S(2)}) collective-permute-start(bf16[3,48,4096]{2,1,0:T(8,128)(2,1)S(1)} %near.1.near_ref), channel_id=1, source_target_pairs={{0,4},{4,0},{8,12},{12,8},{16,20},{20,16},{24,28},{28,24},{32,36},... | collective-permute-start | bytes 3538952 | tf_op jit(solution)/shard_map/ppermute | solution.py:409
